TPU v7x, 32 devices: a whole 2x2x4 slice. The times are simulated.
32 devices in a mesh: seq: 4 (over z), batch: 8 (over y, x, core).
Axes of the slice: x: 2, y: 2, z: 4, core: 2. Of those that a mesh axis runs over, the one named last changes fastest.
Arguments:
- tokens: bfloat16 [8, 1024, 1024], P('batch', 'seq'), may hold values from -6 to 6
- cotangent: bfloat16 [8, 1024, 1024], P('batch', 'seq'), may hold values from -6 to 6
- group_ids: int32 [8], P('batch'), may hold values from 0 to 3
- loss_weight: float32 [4], replicated, may hold values from 0.5 to 2
- gain_attn: bfloat16 [1024], replicated, may hold values from 0.5 to 1.5
- w_query: bfloat16 [1024, 1024], P(('seq', 'batch')), may hold values from -0.1875 to 0.1875
- w_latent: bfloat16 [1024, 512], P(('seq', 'batch')), may hold values from -0.1875 to 0.1875
- w_key_up: bfloat16 [2, 256, 512], replicated, may hold values from -0.375 to 0.375
- w_value_up: bfloat16 [2, 256, 512], replicated, may hold values from -0.375 to 0.375
- w_out: bfloat16 [1024, 1024], P(None, ('seq', 'batch')), may hold values from -0.75 to 0.75
- gain_mlp: bfloat16 [1024], replicated, may hold values from 0.5 to 1.5
- w_gate: bfloat16 [1024, 2816], P(('seq', 'batch')), may hold values from -0.1875 to 0.1875
- w_up: bfloat16 [1024, 2816], P(('seq', 'batch')), may hold values from -0.1875 to 0.1875
- w_down: bfloat16 [2816, 1024], P(('seq', 'batch')), may hold values from -0.109375 to 0.109375
Outputs:
- output: bfloat16 [8, 1024, 1024], P('batch', 'seq')
- input_grad: bfloat16 [8, 1024, 1024], P('batch', 'seq')
- grad_gain_attn: float32 [1024], replicated
- grad_w_query: float32 [1024, 1024], P(('seq', 'batch'))
- grad_w_latent: float32 [1024, 512], P(('seq', 'batch'))
- grad_w_key_up: float32 [2, 256, 512], replicated
- grad_w_value_up: float32 [2, 256, 512], replicated
- grad_w_out: float32 [1024, 1024], P(None, ('seq', 'batch'))
- grad_gain_mlp: float32 [1024], replicated
- grad_w_gate: float32 [1024, 2816], P(('seq', 'batch'))
- grad_w_up: float32 [1024, 2816], P(('seq', 'batch'))
- grad_w_down: float32 [2816, 1024], P(('seq', 'batch'))
All inputs are finite; a program needn't handle non-finite values.
Results may differ from a plain program's by a relative error of at most 0.02.
Values may be sent and summed in bfloat16 or wider, within the bound.
No kernel may reach another device: no remote copies, remote signals or barrier semaphores. Data moves between devices by JAX's collectives and lax.ppermute only.
A program may use at most 256 MiB of HBM per device.

v0:
```python
import jax
import jax.numpy as jnp
from jax import lax
from jax.sharding import PartitionSpec as P

HEADS = 16
HEAD_DIM = 64
LATENT = 256
KV_GROUPS = 2
GROUPS = 4


EPSILON = 1e-06
CONTRACT_ROWS = (((0,), (0,)), ((), ()))
CONTRACT_COLS = (((1,), (1,)), ((), ()))


def rms_scale(values):
    return lax.rsqrt(jnp.mean(values * values, axis=-1, keepdims=True) + EPSILON)


def rms_back(grad_normed, inputs, inv_rms, gain_full):
    weighted = grad_normed * gain_full
    return inv_rms * weighted - inputs * inv_rms**3 * jnp.mean(
        weighted * inputs, axis=-1, keepdims=True
    )


def split_pair(values):
    upper_part = values.astype(jnp.bfloat16)
    lower_part = (values - upper_part.astype(jnp.float32)).astype(jnp.bfloat16)
    return (upper_part, lower_part)


def on_device(
    tokens,
    cotangent,
    group_ids,
    loss_weight,
    gain_attn,
    w_query,
    w_latent,
    w_key_up,
    w_value_up,
    w_out,
    gain_mlp,
    w_gate,
    w_up,
    w_down,
):
    inputs = tokens[0].astype(jnp.float32)
    local_len = inputs.shape[0]
    full_len = local_len * lax.axis_size("seq")
    scale = HEAD_DIM ** (-0.5)
    head_span = 2 * HEAD_DIM
    heads_group = HEADS // KV_GROUPS
    gain_one = gain_attn.astype(jnp.float32)
    gain_two = gain_mlp.astype(jnp.float32)
    query_w, latent_w, out_w = (
        lax.all_gather(w_query, ("seq", "batch"), axis=0, tiled=True),
        lax.all_gather(w_latent, ("seq", "batch"), axis=0, tiled=True),
        lax.all_gather(w_out, ("seq", "batch"), axis=1, tiled=True),
    )
    inv_one = rms_scale(inputs)
    normed_one = (inputs * inv_one * gain_one).astype(jnp.bfloat16)
    queries = jnp.dot(normed_one, query_w, preferred_element_type=jnp.float32).astype(jnp.bfloat16)
    latent = jnp.dot(normed_one, latent_w, preferred_element_type=jnp.float32).astype(jnp.bfloat16)
    latent_all = lax.all_gather(latent, "seq", axis=0, tiled=True)
    latent_grouped = latent_all.reshape(full_len, KV_GROUPS, LATENT)
    key_all = (
        jnp.einsum("lgr,grn->lgn", latent_grouped, w_key_up, preferred_element_type=jnp.float32)
        .astype(jnp.bfloat16)
        .reshape(full_len, HEADS * HEAD_DIM)
    )
    value_all = (
        jnp.einsum("lgr,grn->lgn", latent_grouped, w_value_up, preferred_element_type=jnp.float32)
        .astype(jnp.bfloat16)
        .reshape(full_len, HEADS * HEAD_DIM)
    )
    query_pos = lax.axis_index("seq") * local_len + jnp.arange(local_len, dtype=jnp.int32)
    key_pos = jnp.arange(full_len, dtype=jnp.int32)
    allowed = key_pos[None, :] <= query_pos[:, None]

    def pair_scores(pair_index):
        first = pair_index * head_span
        query_pair = queries[:, first : first + head_span].reshape(local_len, 2, HEAD_DIM)
        key_pair = key_all[:, first : first + head_span].reshape(full_len, 2, HEAD_DIM)
        value_pair = value_all[:, first : first + head_span].reshape(full_len, 2, HEAD_DIM)
        raw_scores = (
            jnp.einsum("ihd,jhd->hij", query_pair, key_pair, preferred_element_type=jnp.float32)
            * scale
        )
        return (jnp.where(allowed[None], raw_scores, -1e30), query_pair, key_pair, value_pair)

    attended_parts = []
    log_totals = []
    for pair_index in range(HEADS // 2):
        scores, query_pair, key_pair, value_pair = pair_scores(pair_index)
        row_max = jnp.max(scores, axis=-1, keepdims=True)
        exponent = jnp.exp(scores - row_max)
        row_total = jnp.sum(exponent, axis=-1, keepdims=True)
        probability = exponent / row_total
        log_totals.append(row_max + jnp.log(row_total))
        mixed = jnp.einsum(
            "hij,jhd->ihd",
            probability.astype(jnp.bfloat16),
            value_pair,
            preferred_element_type=jnp.float32,
        )
        attended_parts.append(mixed.astype(jnp.bfloat16).reshape(local_len, head_span))
    attended = jnp.concatenate(attended_parts, axis=1)
    resid = inputs + jnp.dot(attended, out_w, preferred_element_type=jnp.float32)
    inv_two = rms_scale(resid)
    normed_two = (resid * inv_two * gain_two).astype(jnp.bfloat16)
    gate_w, up_w, down_w = (
        lax.all_gather(w_gate, ("seq", "batch"), axis=0, tiled=True),
        lax.all_gather(w_up, ("seq", "batch"), axis=0, tiled=True),
        lax.all_gather(w_down, ("seq", "batch"), axis=0, tiled=True),
    )
    gate = jnp.dot(normed_two, gate_w, preferred_element_type=jnp.float32)
    up_value = jnp.dot(normed_two, up_w, preferred_element_type=jnp.float32)
    sigma = jax.nn.sigmoid(gate)
    silu_gate = gate * sigma
    hidden = (silu_gate * up_value).astype(jnp.bfloat16)
    mlp_out = jnp.dot(hidden, down_w, preferred_element_type=jnp.float32)
    result = (resid + mlp_out).astype(jnp.bfloat16)[None]
    onehot = (group_ids[:, None] == jnp.arange(GROUPS, dtype=jnp.int32)[None, :]).astype(
        jnp.float32
    )
    counts = lax.psum(jnp.sum(onehot, axis=0), "batch")
    own_count = jnp.sum(onehot[0] * counts)
    own_weight = jnp.sum(onehot[0] * loss_weight)
    total_seqs = lax.axis_size("batch") * group_ids.shape[0]
    seq_factor = own_weight * (total_seqs / GROUPS) / own_count
    grad_out = cotangent[0].astype(jnp.float32) * seq_factor
    grad_out_low = grad_out.astype(jnp.bfloat16)
    back_gate_w, back_up_w, back_down_w = (gate_w, up_w, down_w)
    grad_hidden = lax.dot_general(
        grad_out_low, back_down_w, CONTRACT_COLS, preferred_element_type=jnp.float32
    )
    grad_gate = (grad_hidden * up_value * sigma * (1.0 + gate * (1.0 - sigma))).astype(jnp.bfloat16)
    grad_upval = (grad_hidden * silu_gate).astype(jnp.bfloat16)
    grad_normed_two = lax.dot_general(
        grad_gate, back_gate_w, CONTRACT_COLS, preferred_element_type=jnp.float32
    )
    grad_normed_two = grad_normed_two + lax.dot_general(
        grad_upval, back_up_w, CONTRACT_COLS, preferred_element_type=jnp.float32
    )
    grad_gain_two = jnp.sum(grad_normed_two * resid * inv_two, axis=0)
    grad_resid = grad_out + rms_back(grad_normed_two, resid, inv_two, gain_two)
    grad_resid_low = grad_resid.astype(jnp.bfloat16)
    grad_attended = lax.dot_general(
        grad_resid_low, out_w, CONTRACT_COLS, preferred_element_type=jnp.float32
    ).astype(jnp.bfloat16)
    grad_query_parts = []
    grad_latent_parts = [
        jnp.zeros((full_len, LATENT), jnp.float32) for group_index in range(KV_GROUPS)
    ]
    key_up_parts = [[] for group_index in range(KV_GROUPS)]
    value_up_parts = [[] for group_index in range(KV_GROUPS)]
    for pair_index in range(HEADS // 2):
        scores, query_pair, key_pair, value_pair = pair_scores(pair_index)
        probability = jnp.exp(scores - log_totals[pair_index])
        first = pair_index * head_span
        grad_pair = grad_attended[:, first : first + head_span].reshape(local_len, 2, HEAD_DIM)
        grad_prob = jnp.einsum(
            "ihd,jhd->hij", grad_pair, value_pair, preferred_element_type=jnp.float32
        )
        inner = jnp.sum(probability * grad_prob, axis=-1, keepdims=True)
        grad_scores = (probability * (grad_prob - inner)).astype(jnp.bfloat16)
        grad_query_pair = (
            jnp.einsum("hij,jhd->ihd", grad_scores, key_pair, preferred_element_type=jnp.float32)
            * scale
        )
        grad_query_parts.append(grad_query_pair.reshape(local_len, head_span))
        grad_key_pair = (
            jnp.einsum("hij,ihd->jhd", grad_scores, query_pair, preferred_element_type=jnp.float32)
            * scale
        )
        grad_value_pair = jnp.einsum(
            "hij,ihd->jhd",
            probability.astype(jnp.bfloat16),
            grad_pair,
            preferred_element_type=jnp.float32,
        )
        key_upper, key_lower = split_pair(grad_key_pair)
        value_upper, value_lower = split_pair(grad_value_pair)
        group_index = 2 * pair_index // heads_group
        inside = 2 * pair_index % heads_group * HEAD_DIM
        key_slice = w_key_up[group_index, :, inside : inside + head_span].reshape(
            LATENT, 2, HEAD_DIM
        )
        value_slice = w_value_up[group_index, :, inside : inside + head_span].reshape(
            LATENT, 2, HEAD_DIM
        )
        latent_term = jnp.einsum(
            "jhd,rhd->jr", key_upper, key_slice, preferred_element_type=jnp.float32
        )
        latent_term = latent_term + jnp.einsum(
            "jhd,rhd->jr", key_lower, key_slice, preferred_element_type=jnp.float32
        )
        latent_term = latent_term + jnp.einsum(
            "jhd,rhd->jr", value_upper, value_slice, preferred_element_type=jnp.float32
        )
        latent_term = latent_term + jnp.einsum(
            "jhd,rhd->jr", value_lower, value_slice, preferred_element_type=jnp.float32
        )
        grad_latent_parts[group_index] = grad_latent_parts[group_index] + latent_term
        latent_group = latent_grouped[:, group_index, :]
        key_term = jnp.einsum(
            "jr,jhd->rhd", latent_group, key_upper, preferred_element_type=jnp.float32
        ) + jnp.einsum("jr,jhd->rhd", latent_group, key_lower, preferred_element_type=jnp.float32)
        value_term = jnp.einsum(
            "jr,jhd->rhd", latent_group, value_upper, preferred_element_type=jnp.float32
        ) + jnp.einsum("jr,jhd->rhd", latent_group, value_lower, preferred_element_type=jnp.float32)
        key_up_parts[group_index].append(key_term.reshape(LATENT, head_span))
        value_up_parts[group_index].append(value_term.reshape(LATENT, head_span))
    grad_latent_local = jnp.stack(grad_latent_parts, axis=1).reshape(full_len, KV_GROUPS * LATENT)
    grad_latent = lax.psum_scatter(
        grad_latent_local.astype(jnp.bfloat16), "seq", scatter_dimension=0, tiled=True
    )
    grad_key_up = jnp.stack(
        [jnp.concatenate(key_up_parts[group_index], axis=1) for group_index in range(KV_GROUPS)],
        axis=0,
    )
    grad_value_up = jnp.stack(
        [jnp.concatenate(value_up_parts[group_index], axis=1) for group_index in range(KV_GROUPS)],
        axis=0,
    )
    grad_queries = jnp.concatenate(grad_query_parts, axis=1).astype(jnp.bfloat16)
    grad_normed_one = lax.dot_general(
        grad_queries, query_w, CONTRACT_COLS, preferred_element_type=jnp.float32
    )
    grad_normed_one = grad_normed_one + lax.dot_general(
        grad_latent, latent_w, CONTRACT_COLS, preferred_element_type=jnp.float32
    )
    grad_gain_one = jnp.sum(grad_normed_one * inputs * inv_one, axis=0)
    input_grad = (grad_resid + rms_back(grad_normed_one, inputs, inv_one, gain_one)).astype(
        jnp.bfloat16
    )[None]
    cols_normed_one, cols_normed_two, cols_resid, cols_hidden = (
        lax.all_to_all(normed_one, "seq", split_axis=1, concat_axis=0, tiled=True),
        lax.all_to_all(normed_two, "seq", split_axis=1, concat_axis=0, tiled=True),
        lax.all_to_all(grad_resid_low, "seq", split_axis=1, concat_axis=0, tiled=True),
        lax.all_to_all(hidden, "seq", split_axis=1, concat_axis=0, tiled=True),
    )
    full_gate, full_up, full_out, full_queries, full_latent, full_attended = (
        lax.all_gather(grad_gate, "seq", axis=0, tiled=True),
        lax.all_gather(grad_upval, "seq", axis=0, tiled=True),
        lax.all_gather(grad_out_low, "seq", axis=0, tiled=True),
        lax.all_gather(grad_queries, "seq", axis=0, tiled=True),
        lax.all_gather(grad_latent, "seq", axis=0, tiled=True),
        lax.all_gather(attended, "seq", axis=0, tiled=True),
    )
    rows_gate = lax.dot_general(
        cols_normed_two, full_gate, CONTRACT_ROWS, preferred_element_type=jnp.float32
    )
    rows_up = lax.dot_general(
        cols_normed_two, full_up, CONTRACT_ROWS, preferred_element_type=jnp.float32
    )
    rows_down = lax.dot_general(
        cols_hidden, full_out, CONTRACT_ROWS, preferred_element_type=jnp.float32
    )
    rows_query = lax.dot_general(
        cols_normed_one, full_queries, CONTRACT_ROWS, preferred_element_type=jnp.float32
    )
    rows_latent = lax.dot_general(
        cols_normed_one, full_latent, CONTRACT_ROWS, preferred_element_type=jnp.float32
    )
    cols_out = lax.dot_general(
        full_attended, cols_resid, CONTRACT_ROWS, preferred_element_type=jnp.float32
    )
    owned_gate, owned_up, owned_down, owned_query, owned_latent, owned_out = (
        lax.psum_scatter(
            rows_gate.astype(jnp.bfloat16), "batch", scatter_dimension=0, tiled=True
        ).astype(jnp.float32),
        lax.psum_scatter(
            rows_up.astype(jnp.bfloat16), "batch", scatter_dimension=0, tiled=True
        ).astype(jnp.float32),
        lax.psum_scatter(
            rows_down.astype(jnp.bfloat16), "batch", scatter_dimension=0, tiled=True
        ).astype(jnp.float32),
        lax.psum_scatter(
            rows_query.astype(jnp.bfloat16), "batch", scatter_dimension=0, tiled=True
        ).astype(jnp.float32),
        lax.psum_scatter(
            rows_latent.astype(jnp.bfloat16), "batch", scatter_dimension=0, tiled=True
        ).astype(jnp.float32),
        lax.psum_scatter(
            cols_out.astype(jnp.bfloat16), "batch", scatter_dimension=1, tiled=True
        ).astype(jnp.float32),
    )
    total_gain_one, total_gain_two, total_key_up, total_value_up = lax.psum(
        (grad_gain_one, grad_gain_two, grad_key_up, grad_value_up), ("seq", "batch")
    )
    return (
        result,
        input_grad,
        total_gain_one,
        owned_query,
        owned_latent,
        total_key_up,
        total_value_up,
        owned_out,
        total_gain_two,
        owned_gate,
        owned_up,
        owned_down,
    )


def solution(mesh):
    in_specs = (
        P("batch", "seq", None),
        P("batch", "seq", None),
        P("batch"),
        P(),
        P(),
        P(("seq", "batch"), None),
        P(("seq", "batch"), None),
        P(),
        P(),
        P(None, ("seq", "batch")),
        P(),
        P(("seq", "batch"), None),
        P(("seq", "batch"), None),
        P(("seq", "batch"), None),
    )
    out_specs = (
        P("batch", "seq", None),
        P("batch", "seq", None),
        P(),
        P(("seq", "batch"), None),
        P(("seq", "batch"), None),
        P(),
        P(),
        P(None, ("seq", "batch")),
        P(),
        P(("seq", "batch"), None),
        P(("seq", "batch"), None),
        P(("seq", "batch"), None),
    )
    return jax.shard_map(
        on_device, mesh=mesh, in_specs=in_specs, out_specs=out_specs, check_vma=False
    )
```

profile of v0, /device:TPU:9, one launch (start us, length us, event | category | flops | bytes accessed | tf_op | source)
XLA Modules:
  0.0 1369.0 jit_solution(15700523092011871969)
XLA Ops:
  10.5 54.9 %all-gather.14.cloned.1.call-done = bf16[1024,512]{1,0:T(8,128)(2,1)} async-done(((bf16[32,512]{1,0:T(8,128)(2,1)}), bf16[1024,512]{1,0:T(8,128)(2,1)}) %all-gather.14.cloned.1.call-update) | async-done | bytes 1048592 | tf_op jit(solution)/shard_map/all_gather | solution.py:61
  72.3 11.8 psum.35
  104.3 49.4 %all-gather.18.cloned.1.call-done = bf16[1024,1024]{1,0:T(8,128)(2,1)} async-done(((bf16[32,1024]{1,0:T(8,128)(2,1)}), bf16[1024,1024]{1,0:T(8,128)(2,1)}) %all-gather.18.cloned.1.call-update) | async-done | bytes 2097168 | tf_op jit(solution)/shard_map/all_gather | solution.py:60
  182.7 29.1 %all-gather.20.cloned.1.call-done = bf16[1024,1024]{0,1:T(8,128)(2,1)} async-done(((bf16[1024,32]{0,1:T(8,128)(2,1)}), bf16[1024,1024]{0,1:T(8,128)(2,1)}) %all-gather.20.cloned.1.call-update) | async-done | bytes 2097168 | tf_op jit(solution)/shard_map/all_gather | solution.py:62
  217.6 64.5 %all-gather.22.cloned.1.call-done = bf16[1024,2816]{1,0:T(8,128)(2,1)} async-done(((bf16[32,2816]{1,0:T(8,128)(2,1)}), bf16[1024,2816]{1,0:T(8,128)(2,1)}) %all-gather.22.cloned.1.call-update) | async-done | bytes 5767184 | tf_op jit(solution)/shard_map/all_gather | solution.py:116
  287.9 63.1 %all-gather.24.cloned.1.call-done = bf16[1024,2816]{1,0:T(8,128)(2,1)} async-done(((bf16[32,2816]{1,0:T(8,128)(2,1)}), bf16[1024,2816]{1,0:T(8,128)(2,1)}) %all-gather.24.cloned.1.call-update) | async-done | bytes 5767184 | tf_op jit(solution)/shard_map/all_gather | solution.py:117
  357.1 63.0 %all-gather.26.cloned.1.call-done = bf16[2816,1024]{1,0:T(8,128)(2,1)} async-done(((bf16[88,1024]{1,0:T(8,128)(2,1)}), bf16[2816,1024]{1,0:T(8,128)(2,1)}) %all-gather.26.cloned.1.call-update) | async-done | bytes 5767184 | tf_op jit(solution)/shard_map/all_gather | solution.py:118
  420.1 9.8 multiply_convert_fusion
  534.3 14.1 %reduce-scatter.8.cloned.1.call-done = bf16[256,512]{0,1:T(8,128)(2,1)} async-done(((bf16[1024,512]{0,1:T(8,128)(2,1)}), bf16[256,512]{0,1:T(8,128)(2,1)}) %reduce-scatter.8.cloned.1.call-update) | async-done | bytes 262160 | tf_op jit(solution)/shard_map/reduce_scatter | solution.py:219
  560.3 16.6 %all-to-all-done = bf16[256,4,256]{2,0,1:T(8,128)(2,1)S(1)} async-done(((bf16[256,4,256]{2,0,1:T(8,128)(2,1)}), bf16[256,4,256]{2,0,1:T(8,128)(2,1)S(1)}, u32[]{:S(2)}, u32[]{:S(2)}) %all-to-all-start) | async-done | bytes 524320 | tf_op jit(solution)/shard_map/all_to_all | solution.py:242
  576.9 7.8 all-to-all-start.1
  590.3 7.8 all-to-all-done.1
  598.1 13.5 all-to-all-start.3
  623.8 55.2 %all-gather.28.cloned.1.call-done = bf16[1024,1024]{0,1:T(8,128)(2,1)} async-done(((bf16[256,1024]{0,1:T(8,128)(2,1)}), bf16[1024,1024]{0,1:T(8,128)(2,1)}) %all-gather.28.cloned.1.call-update) | async-done | bytes 2097168 | tf_op jit(solution)/shard_map/all_gather | solution.py:251
  694.5 28.2 %all-gather.30.cloned.1.call-done = bf16[1024,512]{0,1:T(8,128)(2,1)} async-done(((bf16[256,512]{0,1:T(8,128)(2,1)}), bf16[1024,512]{0,1:T(8,128)(2,1)}) %all-gather.30.cloned.1.call-update) | async-done | bytes 1048592 | tf_op jit(solution)/shard_map/all_gather | solution.py:252
  725.1 45.2 %all-gather.38.cloned.1.call-done = bf16[1024,1024]{1,0:T(8,128)(2,1)} async-done(((bf16[256,1024]{1,0:T(8,128)(2,1)}), bf16[1024,1024]{1,0:T(8,128)(2,1)}) %all-gather.38.cloned.1.call-update) | async-done | bytes 2097168 | tf_op jit(solution)/shard_map/all_gather | solution.py:250
  783.7 93.0 %all-gather.34.cloned.1.call-done = bf16[1024,2816]{1,0:T(8,128)(2,1)} async-done(((bf16[256,2816]{1,0:T(8,128)(2,1)}), bf16[1024,2816]{1,0:T(8,128)(2,1)}) %all-gather.34.cloned.1.call-update) | async-done | bytes 5767184 | tf_op jit(solution)/shard_map/all_gather | solution.py:248
  888.6 94.5 %all-gather.36.cloned.1.call-done = bf16[1024,2816]{1,0:T(8,128)(2,1)} async-done(((bf16[256,2816]{1,0:T(8,128)(2,1)}), bf16[1024,2816]{1,0:T(8,128)(2,1)}) %all-gather.36.cloned.1.call-update) | async-done | bytes 5767184 | tf_op jit(solution)/shard_map/all_gather | solution.py:249
  1025.2 39.6 %all-reduce = (f32[1024]{0:T(1024)}, f32[1024]{0:T(1024)}) all-reduce(f32[1024]{0:T(1024)S(1)} %get-tuple-element.14, f32[1024]{0:T(1024)S(1)} %copy-done.270), channel_id=1, replica_groups=mesh['seq'=4,'batch'=8] {'seq','batch'}, use_global_device_ids=true, to_apply=%region_33.34 | all-reduce | flops 2048 | bytes 16384 | tf_op jit(solution)/shard_map/psum | solution.py:293
  1068.7 27.6 %reduce-scatter.12.cloned.1.call-done = bf16[32,512]{1,0:T(8,128)(2,1)} async-done(((bf16[256,512]{1,0:T(8,128)(2,1)}), bf16[32,512]{1,0:T(8,128)(2,1)}) %reduce-scatter.12.cloned.1.call-update) | async-done | bytes 32784 | tf_op jit(solution)/shard_map/reduce_scatter | solution.py:286
  1097.6 40.1 %reduce-scatter.20.cloned.1.call-done = bf16[88,1024]{1,0:T(8,128)(2,1)} async-done(((bf16[704,1024]{1,0:T(8,128)(2,1)}), bf16[88,1024]{1,0:T(8,128)(2,1)}) %reduce-scatter.20.cloned.1.call-update) | async-done | bytes 180240 | tf_op jit(solution)/shard_map/reduce_scatter | solution.py:280
  1139.4 39.8 %reduce-scatter.16.cloned.1.call-done = bf16[32,2816]{1,0:T(8,128)(2,1)} async-done(((bf16[256,2816]{1,0:T(8,128)(2,1)}), bf16[32,2816]{1,0:T(8,128)(2,1)}) %reduce-scatter.16.cloned.1.call-update) | async-done | bytes 180240 | tf_op jit(solution)/shard_map/reduce_scatter | solution.py:274
  1180.9 39.3 %reduce-scatter.18.cloned.1.call-done = bf16[32,2816]{1,0:T(8,128)(2,1)} async-done(((bf16[256,2816]{1,0:T(8,128)(2,1)}), bf16[32,2816]{1,0:T(8,128)(2,1)}) %reduce-scatter.18.cloned.1.call-update) | async-done | bytes 180240 | tf_op jit(solution)/shard_map/reduce_scatter | solution.py:277
  1221.9 136.5 %all-reduce.4.cloned.1.call-done = (f32[2,256,512]{2,1,0:T(8,128)}, f32[2,256,512]{2,1,0:T(8,128)}) async-done(((f32[2,256,512]{2,1,0:T(8,128)}, f32[2,256,512]{2,1,0:T(8,128)}), (f32[2,256,512]{2,1,0:T(8,128)}, f32[2,256,512]{2,1,0:T(8,128)})) %all-reduce.4.cloned.1.call-update) | async-done | bytes 2097168 | tf_op jit(solution)/shard_map/psum | solution.py:293
  (874 shorter events, 304.5 us)
Async XLA Ops:
  7.2 58.2 %all-gather.14.cloned.1.call-start = ((), (), s32[]{:S(2)}) async-start(), calls=%async_computation.11 | async-start | bytes 1081344 | tf_op jit(solution)/shard_map/all_gather | solution.py:61
  7.9 91.0 %all-gather.16.cloned.1.call-start = ((), (), s32[]{:S(2)}) async-start(), calls=%async_computation.12 | async-start | bytes 1310720 | tf_op jit(solution)/shard_map/all_gather | solution.py:68
  68.1 85.7 %all-gather.18.cloned.1.call-start = ((), (), s32[]{:S(2)}) async-start(), calls=%async_computation.13 | async-start | bytes 2162688 | tf_op jit(solution)/shard_map/all_gather | solution.py:60
  68.8 142.9 %all-gather.20.cloned.1.call-start = ((), (), s32[]{:S(2)}) async-start(), calls=%async_computation.14 | async-start | bytes 2162688 | tf_op jit(solution)/shard_map/all_gather | solution.py:62
  69.4 212.6 %all-gather.22.cloned.1.call-start = ((), (), s32[]{:S(2)}) async-start(), calls=%async_computation.15 | async-start | bytes 5947392 | tf_op jit(solution)/shard_map/all_gather | solution.py:116
  70.0 281.0 %all-gather.24.cloned.1.call-start = ((), (), s32[]{:S(2)}) async-start(), calls=%async_computation.16 | async-start | bytes 5947392 | tf_op jit(solution)/shard_map/all_gather | solution.py:117
  70.6 349.5 %all-gather.26.cloned.1.call-start = ((), (), s32[]{:S(2)}) async-start(), calls=%async_computation.17 | async-start | bytes 5947392 | tf_op jit(solution)/shard_map/all_gather | solution.py:118
  71.3 477.1 %reduce-scatter.8.cloned.1.call-start = ((), (), s32[]{:S(2)}) async-start(), calls=%async_computation.18 | async-start | bytes 1310720 | tf_op jit(solution)/shard_map/reduce_scatter | solution.py:219
  525.0 93.7 %all-gather.32.cloned.1.call-start = ((), (), s32[]{:S(2)}) async-start(), calls=%async_computation.23 | async-start | bytes 2621440 | tf_op jit(solution)/shard_map/all_gather | solution.py:253
  525.7 153.3 %all-gather.28.cloned.1.call-start = ((), (), s32[]{:S(2)}) async-start(), calls=%async_computation.19 | async-start | bytes 2621440 | tf_op jit(solution)/shard_map/all_gather | solution.py:251
  534.3 188.4 %all-gather.30.cloned.1.call-start = ((), (), s32[]{:S(2)}) async-start(), calls=%async_computation.21 | async-start | bytes 1310720 | tf_op jit(solution)/shard_map/all_gather | solution.py:252
  548.4 221.9 %all-gather.38.cloned.1.call-start = ((), (), s32[]{:S(2)}) async-start(), calls=%async_computation.29 | async-start | bytes 2621440 | tf_op jit(solution)/shard_map/all_gather | solution.py:250
  549.0 327.7 %all-gather.34.cloned.1.call-start = ((), (), s32[]{:S(2)}) async-start(), calls=%async_computation.25 | async-start | bytes 7208960 | tf_op jit(solution)/shard_map/all_gather | solution.py:248
  549.8 433.3 %all-gather.36.cloned.1.call-start = ((), (), s32[]{:S(2)}) async-start(), calls=%async_computation.27 | async-start | bytes 7208960 | tf_op jit(solution)/shard_map/all_gather | solution.py:249
  552.0 24.9 %all-to-all-start = ((bf16[256,4,256]{2,0,1:T(8,128)(2,1)}), bf16[256,4,256]{2,0,1:T(8,128)(2,1)S(1)}, u32[]{:S(2)}, u32[]{:S(2)}) async-start(bf16[256,4,256]{2,0,1:T(8,128)(2,1)} %fusion.88), calls=%async_computation.1 | async-start | bytes 1048576 | tf_op jit(solution)/shard_map/all_to_all | solution.py:242
  598.1 86.8 %all-to-all-start.3 = ((bf16[256,4,704]{0,2,1:T(8,128)(2,1)}), bf16[256,4,704]{0,2,1:T(8,128)(2,1)}, u32[]{:S(2)}, u32[]{:S(2)}) async-start(bf16[256,4,704]{0,2,1:T(8,128)(2,1)} %bitcast.716), calls=%async_computation.9 | async-start | bytes 2883584 | tf_op jit(solution)/shard_map/all_to_all | solution.py:245
  611.5 410.2 %reduce-scatter.14.cloned.1.call-start = ((), (), s32[]{:S(2)}) async-start(), calls=%async_computation.24 | async-start | bytes 589824 | tf_op jit(solution)/shard_map/reduce_scatter | solution.py:289
  622.0 445.2 %reduce-scatter.10.cloned.1.call-start = ((), (), s32[]{:S(2)}) async-start(), calls=%async_computation.20 | async-start | bytes 589824 | tf_op jit(solution)/shard_map/reduce_scatter | solution.py:283
  684.9 98.8 %all-to-all-start.2 = ((bf16[256,4,256]{2,0,1:T(8,128)(2,1)}), bf16[256,4,256]{2,0,1:T(8,128)(2,1)S(1)}, u32[]{:S(2)}, u32[]{:S(2)}) async-start(bf16[256,4,256]{2,0,1:T(8,128)(2,1)} %bitcast.768), calls=%async_computation.6 | async-start | bytes 1048576 | tf_op jit(solution)/shard_map/all_to_all | solution.py:243
  691.8 404.5 %reduce-scatter.12.cloned.1.call-start = ((), (), s32[]{:S(2)}) async-start(), calls=%async_computation.22 | async-start | bytes 294912 | tf_op jit(solution)/shard_map/reduce_scatter | solution.py:286
  725.1 412.6 %reduce-scatter.20.cloned.1.call-start = ((), (), s32[]{:S(2)}) async-start(), calls=%async_computation.30 | async-start | bytes 1622016 | tf_op jit(solution)/shard_map/reduce_scatter | solution.py:280
  775.2 404.0 %reduce-scatter.16.cloned.1.call-start = ((), (), s32[]{:S(2)}) async-start(), calls=%async_computation.26 | async-start | bytes 1622016 | tf_op jit(solution)/shard_map/reduce_scatter | solution.py:274
  882.2 338.0 %reduce-scatter.18.cloned.1.call-start = ((), (), s32[]{:S(2)}) async-start(), calls=%async_computation.28 | async-start | bytes 1622016 | tf_op jit(solution)/shard_map/reduce_scatter | solution.py:277
  988.6 369.8 %all-reduce.4.cloned.1.call-start = ((), (), s32[]{:S(2)}) async-start(), calls=%async_computation.31 | async-start | bytes 4194304 | tf_op jit(solution)/shard_map/psum | solution.py:293
  (274 other events, 2618.1 us)
Sparse Core Ops, SparseCore 0:
  10.9 54.4 all-gather.13
  68.2 26.9 all-gather.15
  98.1 55.6 all-gather.17
  156.5 55.2 all-gather.19
  214.4 67.5 all-gather.21
  284.7 66.2 all-gather.23
  353.8 66.2 all-gather.25
  525.1 23.2 reduce-scatter.7
  550.1 68.5 all-gather.31
  620.2 58.7 all-gather.27
  680.6 41.9 all-gather.29
  724.7 45.5 all-gather.37
  772.0 104.6 all-gather.33
  878.2 104.8 all-gather.35
  986.9 34.7 reduce-scatter.13
  1024.7 34.1 reduce-scatter.9
  1062.6 33.6 reduce-scatter.11
  1099.3 38.2 reduce-scatter.19
  1141.3 37.8 reduce-scatter.15
  1182.3 37.8 reduce-scatter.17
  1226.7 131.7 all-reduce.3
where the time goes:
time: 1380 us; the launch traced here: 1370 us
  waiting for transfers between devices  975 us (71%)
  matrix products  175 us (13%)
  local copies, waits for them, and re-layouts  73.2 us (5%)
  blocking collectives  51.4 us (4%)
  other arithmetic  39.3 us (3%)
  starting transfers between devices  34.6 us (3%)
  between operations  20.1 us (1%)
    psum x1, waiting for transfers between devices, on_device(): lax.psum((grad_gain_one, grad_gain_two, grad_key_up, grad_value_up), ('se...  137 us
    all_gather x1, waiting for transfers between devices, on_device(): lax.all_gather(grad_upval, 'seq', axis=0, tiled=True)  94.5 us
    all_gather x1, waiting for transfers between devices, on_device(): lax.all_gather(grad_gate, 'seq', axis=0, tiled=True)  93 us
    all_gather x1, waiting for transfers between devices, on_device(): lax.all_gather(w_gate, ('seq', 'batch'), axis=0, tiled=True)  64.5 us
    all_gather x1, waiting for transfers between devices, on_device(): lax.all_gather(w_up, ('seq', 'batch'), axis=0, tiled=True)  63.1 us
    all_gather x1, waiting for transfers between devices, on_device(): lax.all_gather(w_down, ('seq', 'batch'), axis=0, tiled=True)  63 us
    all_gather x1, waiting for transfers between devices, on_device(): lax.all_gather(grad_queries, 'seq', axis=0, tiled=True)  55.2 us
    all_gather x1, waiting for transfers between devices, on_device(): lax.all_gather(w_latent, ('seq', 'batch'), axis=0, tiled=True)  54.9 us
  transfers between devices with their start and end apart: 25, of which 21 were waited for; matrix products, arithmetic and copies ran while one was open for 13% of the time, Pallas kernels for 0%

commit v1 on v0

v1 whole, which is shorter than its diff:
```python
import math

import jax
import jax.numpy as jnp
from jax import lax
from jax.experimental import pallas as pl
from jax.experimental.pallas import tpu as pltpu
from jax.sharding import Mesh
from jax.sharding import PartitionSpec as P

HEADS = 16
HEAD_DIM = 64
LATENT = 256
KV_GROUPS = 2
GROUPS = 4
EPSILON = 1e-06
BF16 = jnp.bfloat16
F32 = jnp.float32
ROWS = (((0,), (0,)), ((), ()))
COLS = (((1,), (1,)), ((), ()))
PLAIN = (((1,), (0,)), ((), ()))


def dot(a, b, dims=PLAIN):
    return lax.dot_general(a, b, dims, preferred_element_type=F32)


def shift(values, axis, step):
    size = lax.axis_size(axis)
    return lax.ppermute(values, axis, [(i, (i + step) % size) for i in range(size)])


def swap(values):
    return shift(values, "core", 1)


def spread_z(shard):
    return [shard] + [shift(shard, "z", k) for k in range(1, lax.axis_size("z"))]


def spread_plane(stack, by_x):
    ny, nx = lax.axis_size("y"), lax.axis_size("x")
    blocks = [[None] * nx for _ in range(ny)]
    blocks[0][0] = stack
    for i in range(1, nx):
        blocks[0][i] = shift(stack, "x", i)
    for j in range(1, ny):
        blocks[j][0] = shift(stack, "y", j)
    for j in range(1, ny):
        for i in range(1, nx):
            blocks[j][i] = shift(blocks[j][0], "x", i) if by_x else shift(blocks[0][i], "y", j)
    return blocks


def collect(blocks, by_x):
    ny, nx, nz = lax.axis_size("y"), lax.axis_size("x"), lax.axis_size("z")
    if not by_x:
        blocks = [[blocks[j][i] for j in range(ny)] for i in range(nx)]
        first, second, n_first, n_second = "y", "x", ny, nx
    else:
        first, second, n_first, n_second = "x", "y", nx, ny
    totals = []
    for j in reversed(range(n_second)):
        total = blocks[j][0].astype(F32)
        for i in range(1, n_first):
            total = total + shift(blocks[j][i], first, i).astype(F32)
        totals.append(total)
    own = totals[-1]
    for j in range(1, n_second):
        own = own + shift(totals[n_second - 1 - j].astype(BF16), second, j).astype(F32)
    total = own[0]
    for k in range(1, nz):
        total = total + shift(own[k].astype(BF16), "z", k).astype(F32)
    return total


def place(sizes, offsets):
    return [lax.rem(lax.axis_index(name) + n + o, n) for (name, n), o in zip(sizes, offsets)]


def merge_blocks(blocks):
    ny, nx = len(blocks), len(blocks[0])
    nz, rows, columns = blocks[0][0].shape
    flat = [blocks[j][i] for j in range(ny) for i in range(nx)]
    sizes = (("z", nz), ("y", ny), ("x", nx))

    def kernel(*refs):
        out, sems = refs[-2], refs[-1]
        copies = []
        for j in range(ny):
            for i in range(nx):
                for k in range(nz):
                    z, y, x = place(sizes, (-k, -j, -i))
                    n = j * nx + i
                    copies.append(
                        pltpu.make_async_copy(refs[n].at[k], out.at[z, y, x], sems.at[n * nz + k])
                    )
        for copy in copies:
            copy.start()
        for copy in copies:
            copy.wait()

    out = pl.pallas_call(
        kernel,
        out_shape=jax.ShapeDtypeStruct((nz, ny, nx, rows, columns), flat[0].dtype),
        in_specs=[pl.BlockSpec(memory_space=pl.ANY)] * len(flat),
        out_specs=pl.BlockSpec(memory_space=pl.ANY),
        scratch_shapes=[pltpu.SemaphoreType.DMA((nz * ny * nx,))],
        name="merge",
    )(*flat)
    return out.reshape(nz * ny * nx * rows, columns)


def split_blocks(full):
    nz, ny, nx = lax.axis_size("z"), lax.axis_size("y"), lax.axis_size("x")
    rows = full.shape[0] // (nz * ny * nx)
    columns = full.shape[1]
    sizes = (("z", nz), ("y", ny), ("x", nx))

    def kernel(*refs):
        source, outs, sems = refs[0], refs[1:-1], refs[-1]
        copies = []
        for j in range(ny):
            for i in range(nx):
                for k in range(nz):
                    z, y, x = place(sizes, (k, j, i))
                    n = j * nx + i
                    copies.append(
                        pltpu.make_async_copy(source.at[z, y, x], outs[n].at[k], sems.at[n * nz + k])
                    )
        for copy in copies:
            copy.start()
        for copy in copies:
            copy.wait()

    outs = pl.pallas_call(
        kernel,
        out_shape=[jax.ShapeDtypeStruct((nz, rows, columns), full.dtype)] * (ny * nx),
        in_specs=[pl.BlockSpec(memory_space=pl.ANY)],
        out_specs=[pl.BlockSpec(memory_space=pl.ANY)] * (ny * nx),
        scratch_shapes=[pltpu.SemaphoreType.DMA((nz * ny * nx,))],
        name="split",
    )(full.reshape(nz, ny, nx, rows, columns))
    return [[outs[j * nx + i] for i in range(nx)] for j in range(ny)]


def all_sum(values, axes):
    for axis in axes:
        size = lax.axis_size(axis)
        total = values
        for k in range(1, size):
            total = total + shift(values, axis, k)
        values = total
    return values


def head_halves(pair):
    lane = lax.broadcasted_iota(jnp.int32, pair.shape, 1)
    zero = jnp.zeros_like(pair)
    return jnp.concatenate(
        [jnp.where(lane < HEAD_DIM, pair, zero), jnp.where(lane >= HEAD_DIM, pair, zero)], axis=0
    )


def join_halves(halves):
    rows = halves.shape[0] // 2
    lane = lax.broadcasted_iota(jnp.int32, (rows, halves.shape[1]), 1)
    return jnp.where(lane < HEAD_DIM, halves[:rows], halves[rows:])


def attend_kernel(nz, q_ref, *refs):
    lats, (wk_ref, wv_ref, att_ref, key_ref, value_ref, prob_ref) = refs[:nz], refs[nz:]
    local = q_ref.shape[1]
    z = lax.axis_index("z")
    q2 = head_halves(q_ref[0] * BF16(HEAD_DIM**-0.5))
    wk, wv = wk_ref[...], wv_ref[...]
    scores = []
    for k in range(nz):
        lat = lats[k][0]
        key = dot(lat, wk).astype(BF16)
        value = dot(lat, wv).astype(BF16)
        key_ref[0, k * local : (k + 1) * local] = key
        value_ref[0, k * local : (k + 1) * local] = value
        block = dot(q2, key, COLS)
        if k == 0:
            row = lax.rem(lax.broadcasted_iota(jnp.int32, block.shape, 0), local)
            column = lax.broadcasted_iota(jnp.int32, block.shape, 1)
            block = jnp.where(column <= row, block, -1e30)
        else:
            block = block + jnp.where(z >= k, 0.0, -1e30)
        scores.append(block)
    top = scores[0]
    for block in scores[1:]:
        top = jnp.maximum(top, block)
    top = jnp.max(top, axis=1, keepdims=True)
    exps = [jnp.exp(block - top) for block in scores]
    total = exps[0]
    for block in exps[1:]:
        total = total + block
    inverse = 1.0 / jnp.sum(total, axis=1, keepdims=True)
    mixed = jnp.zeros((2 * local, q_ref.shape[2]), F32)
    for k in range(nz):
        prob = (exps[k] * inverse).astype(BF16)
        prob_ref[0, 0, k] = prob
        mixed = mixed + dot(prob, value_ref[0, k * local : (k + 1) * local])
    att_ref[0] = join_halves(mixed).astype(BF16)


def attend(queries, lats, key_up, value_up):
    seqs, local, width = queries.shape
    nz = len(lats)
    pairs = width // 128
    query_spec = pl.BlockSpec((1, local, 128), lambda s, h: (s, 0, h))
    full_spec = pl.BlockSpec((1, nz * local, 128), lambda s, h: (s, 0, h))
    lat_spec = pl.BlockSpec((1, local, LATENT), lambda s, h: (s, 0, 0))
    up_spec = pl.BlockSpec((LATENT, 128), lambda s, h: (0, h))
    full = jax.ShapeDtypeStruct((seqs, nz * local, width), BF16)
    return pl.pallas_call(
        lambda *refs: attend_kernel(nz, *refs),
        grid=(seqs, pairs),
        in_specs=[query_spec] + [lat_spec] * nz + [up_spec] * 2,
        out_specs=[
            query_spec,
            full_spec,
            full_spec,
            pl.BlockSpec((1, 1, nz, 2 * local, local), lambda s, h: (s, h, 0, 0, 0)),
        ],
        out_shape=[
            jax.ShapeDtypeStruct(queries.shape, BF16),
            full,
            full,
            jax.ShapeDtypeStruct((seqs, pairs, nz, 2 * local, local), BF16),
        ],
        compiler_params=pltpu.CompilerParams(vmem_limit_bytes=48 * 2**20),
        cost_estimate=pl.CostEstimate(
            flops=12 * seqs * pairs * nz * local * local * 256,
            bytes_accessed=16 * 2**20,
            transcendentals=seqs * pairs * nz * 2 * local * local,
        ),
        name="attend",
    )(queries, *lats, key_up, value_up)


def attend_back_kernel(nz, pairs, q_ref, g_ref, att_ref, key_ref, value_ref, prob_ref, *refs):
    lats, (wk_ref, wv_ref), rest = refs[:nz], refs[nz : nz + 2], refs[nz + 2 :]
    dq_ref, dlats, (up_ref, lat_acc) = rest[0], rest[1 : nz + 1], rest[nz + 1 :]
    seq, pair = pl.program_id(0), pl.program_id(1)
    local = q_ref.shape[1]
    scale = HEAD_DIM**-0.5
    q2 = head_halves(q_ref[0] * BF16(scale))
    grad = g_ref[0]
    g2 = head_halves(grad)
    product = grad.astype(F32) * att_ref[0].astype(F32)
    inner = jnp.sum(head_halves(product), axis=1, keepdims=True)
    dq = jnp.zeros((2 * local, 128), F32)
    up_key = jnp.zeros((LATENT, 128), F32)
    up_value = jnp.zeros((LATENT, 128), F32)
    for k in range(nz):
        rows = slice(k * local, (k + 1) * local)
        prob = prob_ref[0, 0, k]
        key, value = key_ref[0, rows], value_ref[0, rows]
        grad_prob = dot(g2, value, COLS)
        grad_score = (prob.astype(F32) * (grad_prob - inner)).astype(BF16)
        dq = dq + dot(grad_score, key)
        grad_key = dot(grad_score, q2, ROWS).astype(BF16)
        grad_value = dot(prob, g2, ROWS).astype(BF16)
        term = dot(grad_key, wk_ref[...], COLS) + dot(grad_value, wv_ref[...], COLS)

        @pl.when(pair == 0)
        def _():
            lat_acc[rows] = term

        @pl.when(pair > 0)
        def _():
            lat_acc[rows] += term

        lat = lats[k][0]
        up_key = up_key + dot(lat, grad_key, ROWS)
        up_value = up_value + dot(lat, grad_value, ROWS)
    dq_ref[0] = (join_halves(dq) * scale).astype(BF16)

    @pl.when(seq == 0)
    def _():
        up_ref[0, pair] = up_key
        up_ref[1, pair] = up_value

    @pl.when(seq > 0)
    def _():
        up_ref[0, pair] += up_key
        up_ref[1, pair] += up_value

    @pl.when(pair == pairs - 1)
    def _():
        for k in range(nz):
            dlats[k][0] = lat_acc[k * local : (k + 1) * local].astype(BF16)


def attend_back(queries, grad_att, attended, keys, values, probs, lats, key_up, value_up):
    seqs, local, width = queries.shape
    nz = len(lats)
    pairs = width // 128
    query_spec = pl.BlockSpec((1, local, 128), lambda s, h: (s, 0, h))
    full_spec = pl.BlockSpec((1, nz * local, 128), lambda s, h: (s, 0, h))
    lat_spec = pl.BlockSpec((1, local, LATENT), lambda s, h: (s, 0, 0))
    up_spec = pl.BlockSpec((LATENT, 128), lambda s, h: (0, h))
    prob_spec = pl.BlockSpec((1, 1, nz, 2 * local, local), lambda s, h: (s, h, 0, 0, 0))
    outs = pl.pallas_call(
        lambda *refs: attend_back_kernel(nz, pairs, *refs),
        grid=(seqs, pairs),
        in_specs=[query_spec] * 3 + [full_spec] * 2 + [prob_spec] + [lat_spec] * nz + [up_spec] * 2,
        out_specs=[query_spec]
        + [lat_spec] * nz
        + [pl.BlockSpec((2, pairs, LATENT, 128), lambda s, h: (0, 0, 0, 0))],
        out_shape=[jax.ShapeDtypeStruct(queries.shape, BF16)]
        + [jax.ShapeDtypeStruct((seqs, local, LATENT), BF16)] * nz
        + [jax.ShapeDtypeStruct((2, pairs, LATENT, 128), F32)],
        scratch_shapes=[pltpu.VMEM((nz * local, LATENT), F32)],
        compiler_params=pltpu.CompilerParams(vmem_limit_bytes=48 * 2**20),
        cost_estimate=pl.CostEstimate(
            flops=24 * seqs * pairs * nz * local * local * 256,
            bytes_accessed=16 * 2**20,
            transcendentals=0,
        ),
        name="attend_back",
    )(queries, grad_att, attended, keys, values, probs, *lats, key_up, value_up)
    return outs[0], outs[1 : nz + 1], outs[nz + 1]


def half(values, which, axis=1):
    size = values.shape[axis] // 2
    return lax.dynamic_slice_in_dim(values, which * size, size, axis)


def in_order(core, own, other, axis):
    return jnp.where(
        core == 0,
        jnp.concatenate([own, other], axis=axis),
        jnp.concatenate([other, own], axis=axis),
    )


def rms_back(grad_normed, inputs, inv_rms, gain):
    weighted = grad_normed * gain
    return inv_rms * weighted - inputs * inv_rms**3 * jnp.mean(
        weighted * inputs, axis=-1, keepdims=True
    )


def inverse_rms(values):
    return lax.rsqrt(jnp.mean(values * values, axis=-1, keepdims=True) + EPSILON)


def on_device(
    tokens,
    cotangent,
    group_ids,
    loss_weight,
    gain_attn,
    w_query,
    w_latent,
    w_key_up,
    w_value_up,
    w_out,
    gain_mlp,
    w_gate,
    w_up,
    w_down,
):
    nz, ny, nx = lax.axis_size("z"), lax.axis_size("y"), lax.axis_size("x")
    core = lax.axis_index("core")
    other = 1 - core
    local, depth = tokens.shape[1:]
    latent_width = w_latent.shape[1] // 2
    hidden_width = w_gate.shape[1] // 2
    query_width = w_query.shape[1] // 2
    gain_one = gain_attn.astype(F32)
    gain_two = gain_mlp.astype(F32)

    out_t = w_out.T
    row_parts = [w_query, w_latent, out_t, w_gate, w_up]
    mine = [half(part, core) for part in row_parts]
    theirs = [half(part, other) for part in row_parts]
    attn_recv = swap(jnp.concatenate(theirs[:3], axis=1))
    attn_shard = in_order(core, jnp.concatenate(mine[:3], axis=1), attn_recv, 0)
    attn_z = jnp.stack(spread_z(attn_shard))
    q_blocks = spread_plane(attn_z[:, :, :query_width], True)
    lo_blocks = spread_plane(attn_z[:, :, query_width:], False)
    ff_recv = swap(jnp.concatenate(theirs[3:], axis=1))
    ff_shard = in_order(core, jnp.concatenate(mine[3:], axis=1), ff_recv, 0)
    down_recv = swap(half(w_down, other))
    down_shard = in_order(core, half(w_down, core), down_recv, 0)
    ff_z = jnp.stack(spread_z(ff_shard))
    gate_blocks = spread_plane(ff_z[:, :, :hidden_width], True)
    up_blocks = spread_plane(ff_z[:, :, hidden_width:], False)
    down_z = jnp.stack(spread_z(down_shard))
    down_blocks = spread_plane(down_z, True)

    both = swap(jnp.concatenate([tokens, cotangent], axis=0))
    inputs = jnp.concatenate([tokens[0], both[0]], axis=0).astype(F32)
    onehot = (group_ids[:, None] == jnp.arange(GROUPS, dtype=jnp.int32)[None, :]).astype(F32)
    onehot_other = swap(onehot)
    counts = all_sum(jnp.sum(onehot, axis=0) + jnp.sum(onehot_other, axis=0), ("x", "y"))
    total_seqs = ny * nx * 2 * group_ids.shape[0]

    def factor(row):
        return jnp.sum(row * loss_weight) * (total_seqs / GROUPS) / jnp.sum(row * counts)

    grad_out = jnp.concatenate(
        [
            cotangent[0].astype(F32) * factor(onehot[0]),
            both[1].astype(F32) * factor(onehot_other[0]),
        ],
        axis=0,
    )
    grad_out_low = grad_out.astype(BF16)

    inv_one = inverse_rms(inputs)
    normed_one = (inputs * inv_one * gain_one).astype(BF16)
    query_w = merge_blocks(q_blocks)
    lo_w = merge_blocks(lo_blocks)
    latent_w, out_w = lo_w[:, :latent_width], lo_w[:, latent_width:]
    latent = dot(normed_one, latent_w).astype(BF16).reshape(2, local, latent_width)
    lats = [latent] + [
        lax.ppermute(latent, "z", [(i, i + k) for i in range(nz - k)]) for k in range(1, nz)
    ]
    queries = dot(normed_one, query_w).astype(BF16).reshape(2, local, query_width)
    key_up = lax.dynamic_index_in_dim(w_key_up, core, 0, keepdims=False)
    value_up = lax.dynamic_index_in_dim(w_value_up, core, 0, keepdims=False)
    attended, keys, values, probs = attend(queries, lats, key_up, value_up)
    attended_flat = attended.reshape(2 * local, query_width)
    partial = dot(attended_flat, out_w, COLS)
    mixed = swap(jnp.concatenate([partial[local:], partial[:local]], axis=0).astype(BF16))
    resid = inputs + partial + mixed.astype(F32)

    inv_two = inverse_rms(resid)
    normed_two = (resid * inv_two * gain_two).astype(BF16)
    gate_w = merge_blocks(gate_blocks)
    up_w = merge_blocks(up_blocks)
    down_cols = merge_blocks(down_blocks)
    down_w = in_order(core, half(down_cols, core, 0), swap(half(down_cols, other, 0)), 1)
    gate = dot(normed_two, gate_w)
    up_value = dot(normed_two, up_w)
    sigma = jax.nn.sigmoid(gate)
    silu_gate = gate * sigma
    hidden = (silu_gate * up_value).astype(BF16)
    mlp_part = dot(hidden, down_w)
    result = (resid[:local] + mlp_part[:local] + swap(mlp_part[local:].astype(BF16)).astype(F32)).astype(
        BF16
    )[None]
    down_rows = dot(hidden, grad_out_low, ROWS).astype(BF16)
    grad_down = in_order(core, half(down_rows, core, 1), swap(half(down_rows, other, 1)), 0)
    down_total = collect(split_blocks(grad_down), True)
    grad_hidden = dot(grad_out_low, down_w, COLS)
    grad_gate = (grad_hidden * up_value * sigma * (1.0 + gate * (1.0 - sigma))).astype(BF16)
    grad_up = (grad_hidden * silu_gate).astype(BF16)
    gate_total = collect(split_blocks(dot(normed_two, grad_gate, ROWS).astype(BF16)), True)
    up_total = collect(split_blocks(dot(normed_two, grad_up, ROWS).astype(BF16)), False)
    normed_part = dot(grad_gate, gate_w, COLS) + dot(grad_up, up_w, COLS)
    gain_two_part = jnp.sum(normed_part * resid * inv_two, axis=0)
    grad_normed = normed_part + swap(
        jnp.concatenate([normed_part[local:], normed_part[:local]], axis=0).astype(BF16)
    ).astype(F32)
    grad_resid = grad_out + rms_back(grad_normed, resid, inv_two, gain_two)
    grad_resid_low = grad_resid.astype(BF16)

    grad_attended = dot(grad_resid_low, out_w).astype(BF16).reshape(2, local, query_width)
    out_rows = dot(grad_resid_low, attended_flat, ROWS).astype(BF16)
    out_total = collect(split_blocks(out_rows), False)
    grad_queries, grad_lats, up_grads = attend_back(
        queries, grad_attended, attended, keys, values, probs, lats, key_up, value_up
    )
    grad_latent = grad_lats[0].astype(F32)
    for k in range(1, nz):
        grad_latent = grad_latent + lax.ppermute(
            grad_lats[k], "z", [(i + k, i) for i in range(nz - k)]
        ).astype(F32)
    grad_latent = grad_latent.astype(BF16).reshape(2 * local, latent_width)
    grad_queries = grad_queries.reshape(2 * local, query_width)
    chips = nz * ny * nx
    up_flat = up_grads.reshape(chips * 16, -1).astype(BF16)
    up_sum = collect(split_blocks(up_flat), True).astype(BF16)
    up_all = merge_blocks(spread_plane(jnp.stack(spread_z(up_sum)), True))
    up_pair = in_order(core, up_all[None], swap(up_all)[None], 0).astype(F32)
    up_pair = up_pair.reshape((2,) + up_grads.shape).transpose(1, 0, 3, 2, 4)
    up_pair = up_pair.reshape(2, KV_GROUPS, LATENT, query_width)

    query_total = collect(split_blocks(dot(normed_one, grad_queries, ROWS).astype(BF16)), True)
    latent_total = collect(split_blocks(dot(normed_one, grad_latent, ROWS).astype(BF16)), False)
    normed_part = dot(grad_queries, query_w, COLS) + dot(grad_latent, latent_w, COLS)
    gain_one_part = jnp.sum(normed_part * inputs * inv_one, axis=0)
    grad_normed = normed_part[:local] + swap(normed_part[local:].astype(BF16)).astype(F32)
    input_grad = (
        grad_resid[:local] + rms_back(grad_normed, inputs[:local], inv_one[:local], gain_one)
    ).astype(BF16)[None]
    gains = all_sum(jnp.stack([gain_one_part, gain_two_part]), ("core", "x", "y", "z"))

    def owned(totals):
        joined = jnp.concatenate(totals, axis=1).astype(BF16)
        received = swap(half(joined, other, 0))
        mine = half(joined, core, 0)
        results, start = [], 0
        for total in totals:
            width = total.shape[1]
            results.append(
                in_order(core, mine[:, start : start + width], received[:, start : start + width], 1)
                .astype(F32)
            )
            start += width
        return results

    (owned_down,) = owned([down_total])
    owned_gate, owned_up = owned([gate_total, up_total])
    owned_out, owned_query, owned_latent = owned([out_total, query_total, latent_total])
    return (
        result,
        input_grad,
        gains[0],
        owned_query,
        owned_latent,
        up_pair[0],
        up_pair[1],
        owned_out.T,
        gains[1],
        owned_gate,
        owned_up,
        owned_down,
    )


def solution(mesh):
    nz = mesh.shape["seq"]
    chips = mesh.shape["batch"] // 2
    nx = math.isqrt(chips)
    while chips % nx:
        nx -= 1
    fine = Mesh(mesh.devices.reshape(nz, chips // nx, nx, 2), ("z", "y", "x", "core"))
    batch = ("y", "x", "core")
    every = ("z",) + batch
    by_rows = P(every, None)
    in_specs = (
        P(batch, "z", None),
        P(batch, "z", None),
        P(batch),
        P(),
        P(),
        by_rows,
        by_rows,
        P(),
        P(),
        P(None, every),
        P(),
        by_rows,
        by_rows,
        by_rows,
    )
    out_specs = (
        P(batch, "z", None),
        P(batch, "z", None),
        P(),
        by_rows,
        by_rows,
        P(),
        P(),
        P(None, every),
        P(),
        by_rows,
        by_rows,
        by_rows,
    )
    return jax.shard_map(
        on_device, mesh=fine, in_specs=in_specs, out_specs=out_specs, check_vma=False
    )
```

time: 1380 us -> 1230 us (0.89)
  waiting for transfers between devices: 975 us -> 159 us
  Pallas kernels: 0 us -> 781 us
  matrix products: 175 us -> 39.4 us
  starting transfers between devices: 34.6 us -> 151 us
  blocking collectives: 51.4 us -> 0 us
  local copies, waits for them, and re-layouts: 73.2 us -> 35.8 us
  between operations: 20.1 us -> 5.69 us
    pallas_call x0 -> x15, Pallas kernels: none -> 781 us  [the longest x7 366 us: split_blocks(): pl.pallas_call(kernel, out_shape=[jax.ShapeDtypeStruct((nz, rows, columns...]
    all_gather x13 -> x0, waiting for transfers between devices: 645 us -> none  [the longest x1 94.5 us: on_device(): lax.all_gather(grad_upval, 'seq', axis=0, tiled=True)]
    reduce_scatter x7 -> x0, waiting for transfers between devices: 163 us -> none  [the longest x1 40.1 us: on_device(): lax.psum_scatter(rows_down.astype(jnp.bfloat16), 'batch', scatter_dimensi...]
    ppermute x0 -> x101, waiting for transfers between devices: none -> 159 us  [the longest x95 143 us: shift(): lax.ppermute(values, axis, [(i, (i + step) % size) for i in range(size)])]
    ppermute x0 -> x101, starting transfers between devices: none -> 151 us  [the longest x95 140 us: shift(): lax.ppermute(values, axis, [(i, (i + step) % size) for i in range(size)])]
    psum x1 -> x0, waiting for transfers between devices: 137 us -> none  [on_device(): lax.psum((grad_gain_one, grad_gain_two, grad_key_up, grad_value_up), ('se...]
    dot_general x100 -> x18, matrix products: 149 us -> 39.4 us  [dot(): return lax.dot_general(a, b, dims, preferred_element_type=F32)]
    psum x2 -> x0, blocking collectives: 51.4 us -> none  [the longest x1 39.6 us: on_device(): lax.psum((grad_gain_one, grad_gain_two, grad_key_up, grad_value_up), ('se...]
  transfers between devices with their start and end apart: 25 -> 101, of which waited for: 21 -> 31; matrix products, arithmetic and copies ran while one was open for 13% -> 8% of each run, Pallas kernels for 0% -> 64%
where the time goes in v1:
time: 1230 us; the launch traced here: 1220 us
  Pallas kernels  781 us (63%)
  waiting for transfers between devices  159 us (13%)
  starting transfers between devices  151 us (12%)
  other arithmetic  44.8 us (4%)
  matrix products  39.4 us (3%)
  local copies, waits for them, and re-layouts  35.8 us (3%)
    pallas_call x7, Pallas kernels, split_blocks(): pl.pallas_call(kernel, out_shape=[jax.ShapeDtypeStruct((nz, rows, columns...  366 us
    pallas_call x6, Pallas kernels, merge_blocks(): pl.pallas_call(kernel, out_shape=jax.ShapeDtypeStruct((nz, ny, nx, rows,...  365 us
    ppermute x95, waiting for transfers between devices, shift(): lax.ppermute(values, axis, [(i, (i + step) % size) for i in range(size)])  143 us
    ppermute x95, starting transfers between devices, shift(): lax.ppermute(values, axis, [(i, (i + step) % size) for i in range(size)])  140 us
    dot_general x18, matrix products, dot(): return lax.dot_general(a, b, dims, preferred_element_type=F32)  39.4 us
    pallas_call x1, Pallas kernels, attend_back(): pl.pallas_call(lambda *refs: attend_back_kernel(nz, pairs, *refs), grid=(...  33.7 us
  transfers between devices with their start and end apart: 101, of which 31 were waited for; matrix products, arithmetic and copies ran while one was open for 8% of the time, Pallas kernels for 64%

profile of v1, /device:TPU:9, one launch (start us, length us, event | category | flops | bytes accessed | tf_op | source)
XLA Modules:
  0.0 1216.2 jit_solution(18212235209586447392)
XLA Ops:
  44.0 15.3 %collective-permute-done.27 = bf16[176,512]{1,0:T(8,128)(2,1)S(1)} collective-permute-done((bf16[176,512]{1,0:T(8,128)(2,1)S(1)}, bf16[176,512]{1,0:T(8,128)(2,1)S(1)}, u32[]{:S(2)}, u32[]{:S(2)}) %collective-permute-start.27) | collective-permute-done | bytes 180256 | tf_op jit(solution)/shard_map/ppermute | solution.py:30
  90.7 33.0 %merge.6 = bf16[4,2,2,64,512]{4,3,2,1,0:T(8,128)(2,1)} custom-call(bf16[4,64,512]{2,1,0:T(8,128)(2,1)} %copy-done.36, bf16[4,64,512]{2,1,0:T(8,128)(2,1)} %copy-done.54, bf16[4,64,512]{2,1,0:T(8,128)(2,1)} %copy-done.53, bf16[4,64,512]{2,1,0:T(8,128)(2,1)} %copy-done.55), custom_call_target="tpu_custom_call" | custom-call | tf_op jit(solution)/shard_map/merge/pallas_call | solution.py:103
  124.5 48.9 %merge.7 = bf16[4,2,2,64,768]{4,3,2,1,0:T(8,128)(2,1)} custom-call(bf16[4,64,768]{2,1,0:T(8,128)(2,1)} %copy-done.31, bf16[4,64,768]{2,1,0:T(8,128)(2,1)} %collective-permute-done.8.refs_1_, bf16[4,64,768]{2,1,0:T(8,128)(2,1)} %collective-permute-done.9.refs_2_, bf16[4,64,768]{2,1,0:T(8,128)(2,1)} %copy-done.47), custom_call_target="tpu_custom_call" | custom-call | tf_op jit(solution)/shard_map/merge/pallas_call | solution.py:103
  184.2 15.7 %collective-permute-done.12.refs_3_.refs_8_ = bf16[2,256,256]{2,1,0:T(8,128)(2,1)S(1)} collective-permute-done((bf16[2,256,256]{2,1,0:T(8,128)(2,1)S(1)}, bf16[2,256,256]{2,1,0:T(8,128)(2,1)S(1)}, u32[]{:S(2)}, u32[]{:S(2)}) %collective-permute-start.12) | collective-permute-done | bytes 262176 | tf_op jit(solution)/shard_map/ppermute | solution.py:424
  201.1 16.3 %attend.1 = (bf16[2,256,512]{2,1,0:T(8,128)(2,1)S(1)}, bf16[2,1024,512]{2,1,0:T(8,128)(2,1)S(1)}, bf16[2,1024,512]{2,1,0:T(8,128)(2,1)}, bf16[2,4,4,512,256]{4,3,2,1,0:T(8,128)(2,1)}) custom-call(bf16[2,256,512]{2,1,0:T(8,128)(2,1)S(1)} %bitcast.231, bf16[2,256,256]{2,1,0:T(8,128)(2,1)S(1)} %bitcast.229, ...), custom_call_target="tpu_custom_call" | custom-call | flops 6442450944 | bytes 16777216 | tf_op jit(solution)/shard_map/attend/pallas_call | solution.py:218
  232.4 88.6 %merge.10 = bf16[4,2,2,176,512]{4,3,2,1,0:T(8,128)(2,1)} custom-call(bf16[4,176,512]{2,1,0:T(8,128)(2,1)} %pad_maximum_fusion.6.refs_0_, bf16[4,176,512]{2,1,0:T(8,128)(2,1)} %collective-permute-done.29.refs_1_, bf16[4,176,512]{2,1,0:T(8,128)(2,1)} %collective-permute-done.30.refs_2_, bf16[4,176,512]{2,1,0:T(8,128)(2,1)} %collective-permute-done.31.refs_3_), custom_call_target="tpu_custom_call" | custom-call | tf_op jit(solution)/shard_map/merge/pallas_call | solution.py:103
  327.4 88.6 %merge.9 = bf16[4,2,2,64,1408]{4,3,2,1,0:T(8,128)(2,1)} custom-call(bf16[4,64,1408]{2,1,0:T(8,128)(2,1)} %get-tuple-element.120.refs_0_, bf16[4,64,1408]{2,1,0:T(8,128)(2,1)} %collective-permute-done.22.refs_1_, bf16[4,64,1408]{2,1,0:T(8,128)(2,1)} %collective-permute-done.23.refs_2_, bf16[4,64,1408]{2,1,0:T(8,128)(2,1)} %collective-permute-done.24.refs_3_), custom_call_target="tpu_custom_call" | custom-call | tf_op jit(solution)/shard_map/merge/pallas_call | solution.py:103
  416.0 88.6 %merge.8 = bf16[4,2,2,64,1408]{4,3,2,1,0:T(8,128)(2,1)} custom-call(bf16[4,64,1408]{2,1,0:T(8,128)(2,1)} %get-tuple-element.119.refs_0_, bf16[4,64,1408]{2,1,0:T(8,128)(2,1)} %collective-permute-done.19.refs_1_, bf16[4,64,1408]{2,1,0:T(8,128)(2,1)} %collective-permute-done.20.refs_2_, bf16[4,64,1408]{2,1,0:T(8,128)(2,1)} %collective-permute-done.21.refs_3_), custom_call_target="tpu_custom_call" | custom-call | tf_op jit(solution)/shard_map/merge/pallas_call | solution.py:103
  538.9 88.6 %split.11 = (bf16[4,64,1408]{2,1,0:T(8,128)(2,1)}, bf16[4,64,1408]{2,1,0:T(8,128)(2,1)}, bf16[4,64,1408]{2,1,0:T(8,128)(2,1)}, bf16[4,64,1408]{2,1,0:T(8,128)(2,1)}) custom-call(bf16[4,2,2,64,1408]{4,3,2,1,0:T(8,128)(2,1)} %bitcast.255), custom_call_target="tpu_custom_call" | custom-call | tf_op jit(solution)/shard_map/split/pallas_call | solution.py:136
  630.9 88.6 %split.12 = (bf16[4,64,1408]{2,1,0:T(8,128)(2,1)}, bf16[4,64,1408]{2,1,0:T(8,128)(2,1)}, bf16[4,64,1408]{2,1,0:T(8,128)(2,1)}, bf16[4,64,1408]{2,1,0:T(8,128)(2,1)}) custom-call(bf16[4,2,2,64,1408]{4,3,2,1,0:T(8,128)(2,1)} %bitcast.252), custom_call_target="tpu_custom_call" | custom-call | tf_op jit(solution)/shard_map/split/pallas_call | solution.py:136
  728.0 9.2 collective-permute-done.87
  744.9 33.7 %attend_back.1 = (bf16[2,256,512]{2,1,0:T(8,128)(2,1)S(1)}, bf16[2,256,256]{2,1,0:T(8,128)(2,1)S(1)}, bf16[2,256,256]{2,1,0:T(8,128)(2,1)S(1)}, bf16[2,256,256]{...) custom-call(bf16[2,256,512]{2,1,0:T(8,128)(2,1)S(1)} %bitcast.232, ...), custom_call_target="tpu_custom_call" | custom-call | flops 12884901888 | bytes 16777216 | tf_op jit(solution)/shard_map/attend_back/pallas_call | solution.py:307
  784.1 17.1 %split.10 = (bf16[4,16,1024]{2,1,0:T(8,128)(2,1)}, bf16[4,16,1024]{2,1,0:T(8,128)(2,1)}, bf16[4,16,1024]{2,1,0:T(8,128)(2,1)}, bf16[4,16,1024]{2,1,0:T(8,128)(2,1)}) custom-call(bf16[4,2,2,16,1024]{4,3,2,1,0:T(8,128)(2,1)} %convert_element_type.493.refs_0_), custom_call_target="tpu_custom_call" | custom-call | tf_op jit(solution)/shard_map/split/pallas_call | solution.py:136
  803.4 33.0 %split.8 = (bf16[4,64,512]{2,1,0:T(8,128)(2,1)}, bf16[4,64,512]{2,1,0:T(8,128)(2,1)}, bf16[4,64,512]{2,1,0:T(8,128)(2,1)}, bf16[4,64,512]{2,1,0:T(8,128)(2,1)}) custom-call(bf16[4,2,2,64,512]{4,3,2,1,0:T(8,128)(2,1)} %bitcast.257), custom_call_target="tpu_custom_call" | custom-call | tf_op jit(solution)/shard_map/split/pallas_call | solution.py:136
  836.4 33.0 %split.7 = (bf16[4,64,512]{2,1,0:T(8,128)(2,1)}, bf16[4,64,512]{2,1,0:T(8,128)(2,1)}, bf16[4,64,512]{2,1,0:T(8,128)(2,1)}, bf16[4,64,512]{2,1,0:T(8,128)(2,1)}) custom-call(bf16[4,2,2,64,512]{4,3,2,1,0:T(8,128)(2,1)} %bitcast.247), custom_call_target="tpu_custom_call" | custom-call | tf_op jit(solution)/shard_map/split/pallas_call | solution.py:136
  904.6 17.1 %split.9 = (bf16[4,64,256]{2,1,0:T(8,128)(2,1)}, bf16[4,64,256]{2,1,0:T(8,128)(2,1)}, bf16[4,64,256]{2,1,0:T(8,128)(2,1)}, bf16[4,64,256]{2,1,0:T(8,128)(2,1)}) custom-call(bf16[4,2,2,64,256]{4,3,2,1,0:T(8,128)(2,1)} %bitcast.268), custom_call_target="tpu_custom_call" | custom-call | tf_op jit(solution)/shard_map/split/pallas_call | solution.py:136
  933.0 9.4 collective-permute-start.93
  968.6 88.6 %split.13 = (bf16[4,176,512]{2,1,0:T(8,128)(2,1)}, bf16[4,176,512]{2,1,0:T(8,128)(2,1)}, bf16[4,176,512]{2,1,0:T(8,128)(2,1)}, bf16[4,176,512]{2,1,0:T(8,128)(2,1)}) custom-call(bf16[4,2,2,176,512]{4,3,2,1,0:T(8,128)(2,1)} %bitcast.242), custom_call_target="tpu_custom_call" | custom-call | tf_op jit(solution)/shard_map/split/pallas_call | solution.py:136
  1080.8 9.6 collective-permute-done.83
  1112.4 10.1 collective-permute-start.92
  1122.6 17.3 %collective-permute-done.78.refs_3_ = bf16[4,16,1024]{2,1,0:T(8,128)(2,1)S(1)} collective-permute-done((bf16[4,16,1024]{2,1,0:T(8,128)(2,1)S(1)}, bf16[4,16,1024]{2,1,0:T(8,128)(2,1)S(1)}, u32[]{:S(2)}, u32[]{:S(2)}) %collective-permute-start.78) | collective-permute-done | bytes 131104 | tf_op jit(solution)/shard_map/ppermute | solution.py:30
  1139.9 8.3 collective-permute-start.66
  1148.2 17.1 %merge.11 = bf16[4,2,2,16,1024]{4,3,2,1,0:T(8,128)(2,1)} custom-call(bf16[4,16,1024]{2,1,0:T(8,128)(2,1)} %copy-done.46, bf16[4,16,1024]{2,1,0:T(8,128)(2,1)} %copy-done.66, bf16[4,16,1024]{2,1,0:T(8,128)(2,1)} %copy-done.65, bf16[4,16,1024]{2,1,0:T(8,128)(2,1)} %copy-done.67), custom_call_target="tpu_custom_call" | custom-call | tf_op jit(solution)/shard_map/merge/pallas_call | solution.py:103
  1173.9 15.2 %collective-permute-done.96 = bf16[4,176,512]{2,1,0:T(8,128)(2,1)S(1)} collective-permute-done((bf16[4,176,512]{2,1,0:T(8,128)(2,1)S(1)}, bf16[4,176,512]{2,1,0:T(8,128)(2,1)S(1)}, u32[]{:S(2)}, u32[]{:S(2)}) %collective-permute-start.96) | collective-permute-done | bytes 720928 | tf_op jit(solution)/shard_map/ppermute | solution.py:30
  (472 shorter events, 319.5 us)
Async XLA Ops:
  65.0 108.4 %collective-permute-start = (bf16[2,256,1024]{2,1,0:T(8,128)(2,1)S(1)}, bf16[2,256,1024]{2,1,0:T(8,128)(2,1)}, u32[]{:S(2)}, u32[]{:S(2)}) collective-permute-start(bf16[2,256,1024]{2,1,0:T(8,128)(2,1)S(1)} %copy-done.35), channel_id=1, source_target_pairs={{0,1},{1,0},{2,3},{3,2},{4,5},{5,4},{6,7},{7,6},{8,9},{9,8},{10,11... | collective-permute-start | bytes 3145736 | tf_op jit(solution)/shard_map/ppermute | solution.py:30
  84.5 142.2 %collective-permute-start.29 = (bf16[4,176,512]{2,1,0:T(8,128)(2,1)}, bf16[4,176,512]{2,1,0:T(8,128)(2,1)}, u32[]{:S(2)}, u32[]{:S(2)}) collective-permute-start(bf16[4,176,512]{2,1,0:T(8,128)(2,1)} %pad_maximum_fusion.6.refs_0_), channel_id=1, source_target_pairs={{0,2},{2,0},{1,3},{3,1},{4,6},{6,4},{5,7},{7,5},{8,10},{10,8},{9,1... | collective-permute-start | bytes 2162696 | tf_op jit(solution)/shard_map/ppermute | solution.py:30
  89.5 93.2 %collective-permute-start.30 = (bf16[4,176,512]{2,1,0:T(8,128)(2,1)}, bf16[4,176,512]{2,1,0:T(8,128)(2,1)}, u32[]{:S(2)}, u32[]{:S(2)}) collective-permute-start(bf16[4,176,512]{2,1,0:T(8,128)(2,1)} %pad_maximum_fusion.6.refs_0_), channel_id=1, source_target_pairs={{0,4},{4,0},{1,5},{5,1},{2,6},{6,2},{3,7},{7,3},{8,12},{12,8},{9,1... | collective-permute-start | bytes 2162696 | tf_op jit(solution)/shard_map/ppermute | solution.py:30
  220.6 284.0 %collective-permute-start.14 = (bf16[512,1024]{1,0:T(8,128)(2,1)}, bf16[512,1024]{1,0:T(8,128)(2,1)}, u32[]{:S(2)}, u32[]{:S(2)}) collective-permute-start(bf16[512,1024]{1,0:T(8,128)(2,1)} %pad_maximum_fusion.4), channel_id=1, source_target_pairs={{0,1},{1,0},{2,3},{3,2},{4,5},{5,4},{6,7},{7,6},{8,9},{9,8},{10,11... | collective-permute-start | bytes 3145736 | tf_op jit(solution)/shard_map/ppermute | solution.py:30
  226.7 98.0 %collective-permute-start.23 = (bf16[4,64,1408]{2,1,0:T(8,128)(2,1)}, bf16[4,64,1408]{2,1,0:T(8,128)(2,1)}, u32[]{:S(2)}, u32[]{:S(2)}) collective-permute-start(bf16[4,64,1408]{2,1,0:T(8,128)(2,1)} %get-tuple-element.120.refs_0_), channel_id=1, source_target_pairs={{0,4},{4,0},{1,5},{5,1},{2,6},{6,2},{3,7},{7,3},{8,12},{12,8},{9,1... | collective-permute-start | bytes 2162696 | tf_op jit(solution)/shard_map/ppermute | solution.py:30
  226.9 189.0 %collective-permute-start.19 = (bf16[4,64,1408]{2,1,0:T(8,128)(2,1)}, bf16[4,64,1408]{2,1,0:T(8,128)(2,1)}, u32[]{:S(2)}, u32[]{:S(2)}) collective-permute-start(bf16[4,64,1408]{2,1,0:T(8,128)(2,1)} %get-tuple-element.119.refs_0_), channel_id=1, source_target_pairs={{0,2},{2,0},{1,3},{3,1},{4,6},{6,4},{5,7},{7,5},{8,10},{10,8},{9,1... | collective-permute-start | bytes 2162696 | tf_op jit(solution)/shard_map/ppermute | solution.py:30
  227.3 100.1 %collective-permute-start.24 = (bf16[4,64,1408]{2,1,0:T(8,128)(2,1)}, bf16[4,64,1408]{2,1,0:T(8,128)(2,1)}, u32[]{:S(2)}, u32[]{:S(2)}) collective-permute-start(bf16[4,64,1408]{2,1,0:T(8,128)(2,1)} %collective-permute-done.22.refs_1_), channel_id=1, source_target_pairs={{0,4},{4,0},{1,5},{5,1},{2,6},{6,2},{3,7},{7,3},{8,12},{12,8},{9,1... | collective-permute-start | bytes 2162696 | tf_op jit(solution)/shard_map/ppermute | solution.py:30
  228.5 187.5 %collective-permute-start.21 = (bf16[4,64,1408]{2,1,0:T(8,128)(2,1)}, bf16[4,64,1408]{2,1,0:T(8,128)(2,1)}, u32[]{:S(2)}, u32[]{:S(2)}) collective-permute-start(bf16[4,64,1408]{2,1,0:T(8,128)(2,1)} %collective-permute-done.20.refs_2_), channel_id=1, source_target_pairs={{0,2},{2,0},{1,3},{3,1},{4,6},{6,4},{5,7},{7,5},{8,10},{10,8},{9,1... | collective-permute-start | bytes 2162696 | tf_op jit(solution)/shard_map/ppermute | solution.py:30
  324.6 186.8 %collective-permute-start.32 = (bf16[1408,512]{1,0:T(8,128)(2,1)}, bf16[1408,512]{1,0:T(8,128)(2,1)}, u32[]{:S(2)}, u32[]{:S(2)}) collective-permute-start(bf16[1408,512]{1,0:T(8,128)(2,1)} %get-tuple-element.116), channel_id=1, source_target_pairs={{0,1},{1,0},{2,3},{3,2},{4,5},{5,4},{6,7},{7,6},{8,9},{9,8},{10,11... | collective-permute-start | bytes 4325384 | tf_op jit(solution)/shard_map/ppermute | solution.py:30
  532.1 191.4 %collective-permute-start.33 = (bf16[256,1024]{1,0:T(8,128)(2,1)}, bf16[256,1024]{1,0:T(8,128)(2,1)}, u32[]{:S(2)}, u32[]{:S(2)}) collective-permute-start(bf16[256,1024]{1,0:T(8,128)(2,1)} %slice.462), channel_id=1, source_target_pairs={{0,1},{1,0},{2,3},{3,2},{4,5},{5,4},{6,7},{7,6},{8,9},{9,8},{10,11... | collective-permute-start | bytes 1572872 | tf_op jit(solution)/shard_map/ppermute | solution.py:30
  627.5 98.2 %collective-permute-start.81 = (bf16[4,64,1408]{2,1,0:T(8,128)(2,1)}, bf16[4,64,1408]{2,1,0:T(8,128)(2,1)}, u32[]{:S(2)}, u32[]{:S(2)}) collective-permute-start(bf16[4,64,1408]{2,1,0:T(8,128)(2,1)} %get-tuple-element.79), channel_id=1, source_target_pairs={{0,2},{2,0},{1,3},{3,1},{4,6},{6,4},{5,7},{7,5},{8,10},{10,8},{9,1... | collective-permute-start | bytes 2162696 | tf_op jit(solution)/shard_map/ppermute | solution.py:30
  628.9 109.4 %collective-permute-start.37 = (bf16[512,1024]{1,0:T(8,128)(2,1)}, bf16[512,1024]{1,0:T(8,128)(2,1)}, u32[]{:S(2)}, u32[]{:S(2)}) collective-permute-start(bf16[512,1024]{1,0:T(8,128)(2,1)} %pad_maximum_fusion.5), channel_id=1, source_target_pairs={{0,1},{1,0},{2,3},{3,2},{4,5},{5,4},{6,7},{7,6},{8,9},{9,8},{10,11... | collective-permute-start | bytes 3145736 | tf_op jit(solution)/shard_map/ppermute | solution.py:30
  629.7 314.0 %collective-permute-start.80 = (bf16[4,64,1408]{2,1,0:T(8,128)(2,1)}, bf16[4,64,1408]{2,1,0:T(8,128)(2,1)}, u32[]{:S(2)}, u32[]{:S(2)}) collective-permute-start(bf16[4,64,1408]{2,1,0:T(8,128)(2,1)} %get-tuple-element.77), channel_id=1, source_target_pairs={{0,2},{2,0},{1,3},{3,1},{4,6},{6,4},{5,7},{7,5},{8,10},{10,8},{9,1... | collective-permute-start | bytes 2162696 | tf_op jit(solution)/shard_map/ppermute | solution.py:30
  778.6 92.2 %collective-permute-start.40 = (bf16[2,256,256]{2,1,0:T(8,128)(2,1)}, bf16[2,256,256]{2,1,0:T(8,128)(2,1)S(1)}, u32[]{:S(2)}, u32[]{:S(2)}) collective-permute-start(bf16[2,256,256]{2,1,0:T(8,128)(2,1)} %get-tuple-element.58), channel_id=1, source_target_pairs={{24,0},{25,1},{26,2},{27,3},{28,4},{29,5},{30,6},{31,7}} | collective-permute-start | bytes 786440 | tf_op jit(solution)/shard_map/ppermute | solution.py:474
  779.4 92.6 %collective-permute-start.39 = (bf16[2,256,256]{2,1,0:T(8,128)(2,1)S(1)}, bf16[2,256,256]{2,1,0:T(8,128)(2,1)}, u32[]{:S(2)}, u32[]{:S(2)}) collective-permute-start(bf16[2,256,256]{2,1,0:T(8,128)(2,1)S(1)} %get-tuple-element.57), channel_id=1, source_target_pairs={{16,0},{24,8},{17,1},{25,9},{18,2},{26,10},{19,3},{27,11},{20,4},{... | collective-permute-start | bytes 786440 | tf_op jit(solution)/shard_map/ppermute | solution.py:474
  780.7 92.6 %collective-permute-start.38 = (bf16[2,256,256]{2,1,0:T(8,128)(2,1)S(1)}, bf16[2,256,256]{2,1,0:T(8,128)(2,1)}, u32[]{:S(2)}, u32[]{:S(2)}) collective-permute-start(bf16[2,256,256]{2,1,0:T(8,128)(2,1)S(1)} %get-tuple-element.56), channel_id=1, source_target_pairs={{8,0},{16,8},{24,16},{9,1},{17,9},{25,17},{10,2},{18,10},{26,18},{... | collective-permute-start | bytes 786440 | tf_op jit(solution)/shard_map/ppermute | solution.py:474
  801.3 68.2 %collective-permute-start.68 = (bf16[4,16,1024]{2,1,0:T(8,128)(2,1)}, bf16[4,16,1024]{2,1,0:T(8,128)(2,1)}, u32[]{:S(2)}, u32[]{:S(2)}) collective-permute-start(bf16[4,16,1024]{2,1,0:T(8,128)(2,1)} %get-tuple-element.75), channel_id=1, source_target_pairs={{0,2},{2,0},{1,3},{3,1},{4,6},{6,4},{5,7},{7,5},{8,10},{10,8},{9,1... | collective-permute-start | bytes 393224 | tf_op jit(solution)/shard_map/ppermute | solution.py:30
  869.5 74.5 %collective-permute-start.82 = (bf16[4,64,1408]{2,1,0:T(8,128)(2,1)S(1)}, bf16[4,64,1408]{2,1,0:T(8,128)(2,1)}, u32[]{:S(2)}, u32[]{:S(2)}) collective-permute-start(bf16[4,64,1408]{2,1,0:T(8,128)(2,1)S(1)} %copy-done.39), channel_id=1, source_target_pairs={{0,4},{4,0},{1,5},{5,1},{2,6},{6,2},{3,7},{7,3},{8,12},{12,8},{9,1... | collective-permute-start | bytes 2162696 | tf_op jit(solution)/shard_map/ppermute | solution.py:30
  943.6 116.3 %collective-permute-start.54 = (bf16[4,64,512]{2,1,0:T(8,128)(2,1)}, bf16[4,64,512]{2,1,0:T(8,128)(2,1)}, u32[]{:S(2)}, u32[]{:S(2)}) collective-permute-start(bf16[4,64,512]{2,1,0:T(8,128)(2,1)} %get-tuple-element.64), channel_id=1, source_target_pairs={{0,2},{2,0},{1,3},{3,1},{4,6},{6,4},{5,7},{7,5},{8,10},{10,8},{9,1... | collective-permute-start | bytes 786440 | tf_op jit(solution)/shard_map/ppermute | solution.py:30
  944.0 119.8 %collective-permute-start.48 = (bf16[4,64,512]{2,1,0:T(8,128)(2,1)}, bf16[4,64,512]{2,1,0:T(8,128)(2,1)}, u32[]{:S(2)}, u32[]{:S(2)}) collective-permute-start(bf16[4,64,512]{2,1,0:T(8,128)(2,1)} %get-tuple-element.60), channel_id=1, source_target_pairs={{0,4},{4,0},{1,5},{5,1},{2,6},{6,2},{3,7},{7,3},{8,12},{12,8},{9,1... | collective-permute-start | bytes 786440 | tf_op jit(solution)/shard_map/ppermute | solution.py:30
  946.7 226.9 %collective-permute-start.41 = (bf16[256,1024]{1,0:T(8,128)(2,1)}, bf16[256,1024]{1,0:T(8,128)(2,1)S(1)}, u32[]{:S(2)}, u32[]{:S(2)}) collective-permute-start(bf16[256,1024]{1,0:T(8,128)(2,1)} %slice.461), channel_id=1, source_target_pairs={{0,1},{1,0},{2,3},{3,2},{4,5},{5,4},{6,7},{7,6},{8,9},{9,8},{10,11... | collective-permute-start | bytes 1572872 | tf_op jit(solution)/shard_map/ppermute | solution.py:30
  964.4 92.8 %collective-permute-start.60 = (bf16[4,64,256]{2,1,0:T(8,128)(2,1)}, bf16[4,64,256]{2,1,0:T(8,128)(2,1)}, u32[]{:S(2)}, u32[]{:S(2)}) collective-permute-start(bf16[4,64,256]{2,1,0:T(8,128)(2,1)} %get-tuple-element.68), channel_id=1, source_target_pairs={{0,4},{4,0},{1,5},{5,1},{2,6},{6,2},{3,7},{7,3},{8,12},{12,8},{9,1... | collective-permute-start | bytes 393224 | tf_op jit(solution)/shard_map/ppermute | solution.py:30
  965.2 93.2 %collective-permute-start.62 = (bf16[4,64,256]{2,1,0:T(8,128)(2,1)}, bf16[4,64,256]{2,1,0:T(8,128)(2,1)}, u32[]{:S(2)}, u32[]{:S(2)}) collective-permute-start(bf16[4,64,256]{2,1,0:T(8,128)(2,1)} %add_convert_fusion.7), channel_id=1, source_target_pairs={{0,2},{2,0},{1,3},{3,1},{4,6},{6,4},{5,7},{7,5},{8,10},{10,8},{9,1... | collective-permute-start | bytes 393224 | tf_op jit(solution)/shard_map/ppermute | solution.py:30
  1110.1 63.8 %collective-permute-start.94 = (bf16[4,176,512]{2,1,0:T(8,128)(2,1)}, bf16[4,176,512]{2,1,0:T(8,128)(2,1)}, u32[]{:S(2)}, u32[]{:S(2)}) collective-permute-start(bf16[4,176,512]{2,1,0:T(8,128)(2,1)} %get-tuple-element.85), channel_id=1, source_target_pairs={{0,2},{2,0},{1,3},{3,1},{4,6},{6,4},{5,7},{7,5},{8,10},{10,8},{9,1... | collective-permute-start | bytes 2162696 | tf_op jit(solution)/shard_map/ppermute | solution.py:30
  (149 other events, 2528.1 us)

commit v2 on v1

v2 whole, which is shorter than its diff:
```python
import math

import jax
import jax.numpy as jnp
from jax import lax
from jax.experimental import pallas as pl
from jax.experimental.pallas import tpu as pltpu
from jax.sharding import Mesh
from jax.sharding import PartitionSpec as P

HEADS = 16
HEAD_DIM = 64
LATENT = 256
KV_GROUPS = 2
GROUPS = 4
EPSILON = 1e-06
BF16 = jnp.bfloat16
F32 = jnp.float32
ROWS = (((0,), (0,)), ((), ()))
OPT = {"attn_plane": 5, "attn_z": 13, "back_0": 112, "back_1": 92, "c_attend": 4, "c_back": 4, "c_fb": 4, "c_ff": 4, "c_merge": 4, "c_mix": 4, "c_rb": 4, "c_split": 4, "down_last": 2, "down_plane": 2, "down_z": 2, "ff_back_z": 1, "ff_plane": 4, "ff_z": 1, "gains": 2, "hidden": 1, "kv": 2, "kv_spread": 4, "kv_z": 3, "lat_back": 16, "normed_last": 1, "normed_part": 1, "query_back": 2}
COLS = (((1,), (1,)), ((), ()))
PLAIN = (((1,), (0,)), ((), ()))


def dot(a, b, dims=PLAIN):
    return lax.dot_general(a, b, dims, preferred_element_type=F32)


PLANE = ("y", "x", "core")


def shift(values, axis, step):
    size = lax.axis_size(axis)
    return lax.ppermute(values, axis, [(i, (i + step) % size) for i in range(size)])


def leg(values, first, step):
    size = lax.axis_size("x")
    pairs = []
    for y in range(size):
        for x in range(size):
            for core in range(2):
                if (core == 0) == first:
                    target = (y, (x + step) % size, core)
                else:
                    target = ((y + step) % size, x, core)
                pairs.append(
                    ((y * size + x) * 2 + core, (target[0] * size + target[1]) * 2 + target[2])
                )
    return lax.ppermute(values, PLANE, pairs)


def swap(values):
    return shift(values, "core", 1)


def spread_z(shard):
    return [shard] + [shift(shard, "z", k) for k in range(1, lax.axis_size("z"))]


def spread_ring(shard):
    nz = lax.axis_size("z")
    pairs = [(z * 2 + c, (z + 1 - 2 * c) % nz * 2 + c) for z in range(nz) for c in range(2)]
    blocks = [shard]
    for _ in range(nz - 1):
        blocks.append(lax.ppermute(blocks[-1], ("z", "core"), pairs))
    return blocks


def spread_own(stack):
    size = lax.axis_size("x")
    return (
        [leg(stack, True, a) for a in range(1, size)],
        [leg(stack, False, b) for b in range(1, size)],
    )


def spread_rest(stack, on_a, on_b):
    size = lax.axis_size("x")
    return [[stack] + on_a] + [
        [on_b[b - 1]] + [leg(block, False, b) for block in on_a] for b in range(1, size)
    ]


def after(value, *others):
    return lax.optimization_barrier((value,) + others)[0]


def tie(name, value, *others):
    mask = OPT.get(name, 0)
    chosen = [other for i, other in enumerate(others) if mask >> i & 1]
    return after(value, *chosen) if chosen else value


def cost(name, flops):
    return pl.CostEstimate(
        flops=int(flops * OPT.get(name, 0) / 4), bytes_accessed=4096, transcendentals=0
    )


def send_b(parts):
    return [leg(parts[b], False, b) for b in range(1, len(parts))]


def add_b(parts, received):
    row = parts[0]
    for part in received:
        row = add(row, part)
    return row


def send_a(row):
    return [leg(row[a], True, a) for a in range(1, row.shape[0])]


def add_a(row, received):
    own = row[0]
    for part in received:
        own = add(own, part)
    return own


def send_z(own):
    return [shift(own[k], "z", k) for k in range(1, own.shape[0])]


def add_z(own, received):
    total = own[0].astype(F32)
    for part in received:
        total = total + part.astype(F32)
    return total


def add(left, right):
    return (left.astype(F32) + right.astype(F32)).astype(BF16)


def to_half(values, step):
    nz = lax.axis_size("z")
    pairs = []
    for z in range(nz):
        keeper = z // (nz // 2)
        source = z * 2 + (keeper if step else 1 - keeper)
        pairs.append((source, (z + step) % nz * 2 + keeper))
    return lax.ppermute(values, ("z", "core"), pairs)


def spread_down_z(chip):
    nz, z, core = lax.axis_size("z"), lax.axis_index("z"), lax.axis_index("core")
    return [chip] + [to_half(chip, k) for k in range(1, nz)]


def down_stack(received):
    nz, z, core = lax.axis_size("z"), lax.axis_index("z"), lax.axis_index("core")
    received = jnp.stack(received)
    parts = []
    for j in range(nz // 2):
        step = lax.rem(z + nz - core * (nz // 2) - j, nz)
        parts.append(lax.dynamic_slice_in_dim(received, step, 1, 0))
    return jnp.concatenate(parts, axis=0)


def down_block(own, chip_z):
    count = own.shape[0]
    index = jnp.clip(chip_z - lax.axis_index("core") * count, 0, count - 1)
    return lax.dynamic_index_in_dim(own, index, 0, keepdims=False)


def send_down_z(own):
    nz, z, count = lax.axis_size("z"), lax.axis_index("z"), own.shape[0]
    received = []
    for k in range(1, nz):
        pairs = [((d + k) % nz * 2 + d // count, d * 2 + d // count) for d in range(nz)]
        part = down_block(own, lax.rem(z + nz - k, nz))
        received.append(lax.ppermute(part, ("z", "core"), pairs))
    return received


def own_down(own, received):
    nz, z, core = lax.axis_size("z"), lax.axis_index("z"), lax.axis_index("core")
    count = nz // 2
    total = down_block(own, z).astype(F32)
    for part in received:
        total = total + part.astype(F32)
    pairs = [(d * 2 + d // count, d * 2 + 1 - d // count) for d in range(nz)]
    sent = lax.ppermute(half(total, 1 - core, 0).astype(BF16), ("z", "core"), pairs)
    return jnp.where(core == z // count, half(total, core, 0), sent.astype(F32))


def place(size, nz, k, b, a):
    core = lax.axis_index("core")
    z = lax.rem(lax.axis_index("z") + nz + k, nz)
    y = lax.rem(lax.axis_index("y") + size + b + core * (a - b), size)
    x = lax.rem(lax.axis_index("x") + size + a + core * (b - a), size)
    return z, y, x


def merge_blocks(blocks, fixed=False, ring=False):
    size = len(blocks)
    nz, rows, columns = blocks[0][0].shape
    parts = [block for row in blocks for block in row]

    def kernel(*refs):
        out, sems = refs[-2], refs[-1]
        copies = []
        for b in range(size):
            for a in range(size):
                for k in range(nz):
                    away = k * (2 * lax.axis_index("core") - 1) if ring else -k
                    z, y, x = place(size, nz, away, -b, -a)
                    n = b * size + a
                    copies.append(
                        pltpu.make_async_copy(
                            refs[n].at[k], out.at[k if fixed else z, y, x], sems.at[n * nz + k]
                        )
                    )
        for copy in copies:
            copy.start()
        for copy in copies:
            copy.wait()

    out = pl.pallas_call(
        kernel,
        out_shape=jax.ShapeDtypeStruct((nz, size, size, rows, columns), parts[0].dtype),
        in_specs=[pl.BlockSpec(memory_space=pl.ANY)] * len(parts),
        out_specs=pl.BlockSpec(memory_space=pltpu.VMEM),
        scratch_shapes=[pltpu.SemaphoreType.DMA((nz * size * size,))],
        compiler_params=pltpu.CompilerParams(vmem_limit_bytes=48 * 2**20),
        cost_estimate=cost("c_merge", 3e9),
        name="merge",
    )(*parts)
    return out.reshape(nz * size * size * rows, columns)


def split_blocks(full, nz, fixed=False):
    size = lax.axis_size("x")
    rows = full.shape[0] // (nz * size * size)
    columns = full.shape[1]

    def kernel(*refs):
        source, outs, sems = refs[0], refs[1:-1], refs[-1]
        copies = []
        for b in range(size):
            for a in range(size):
                for k in range(nz):
                    z, y, x = place(size, nz, k, b, a)
                    copies.append(
                        pltpu.make_async_copy(
                            source.at[k if fixed else z, y, x],
                            outs[b].at[a, k],
                            sems.at[(b * size + a) * nz + k],
                        )
                    )
        for copy in copies:
            copy.start()
        for copy in copies:
            copy.wait()

    return pl.pallas_call(
        kernel,
        out_shape=[jax.ShapeDtypeStruct((size, nz, rows, columns), full.dtype)] * size,
        in_specs=[pl.BlockSpec(memory_space=pltpu.VMEM)],
        out_specs=[pl.BlockSpec(memory_space=pl.ANY)] * size,
        scratch_shapes=[pltpu.SemaphoreType.DMA((nz * size * size,))],
        compiler_params=pltpu.CompilerParams(vmem_limit_bytes=48 * 2**20),
        cost_estimate=cost("c_split", 3e9),
        name="split",
    )(full.reshape(nz, size, size, rows, columns))


def all_sum(values, axes):
    for axis in axes:
        size = lax.axis_size(axis)
        total = values
        for k in range(1, size):
            total = total + shift(values, axis, k)
        values = total
    return values


def head_halves(pair):
    lane = lax.broadcasted_iota(jnp.int32, pair.shape, 1)
    zero = jnp.zeros_like(pair)
    return jnp.concatenate(
        [jnp.where(lane < HEAD_DIM, pair, zero), jnp.where(lane >= HEAD_DIM, pair, zero)], axis=0
    )


def join_halves(halves):
    rows = halves.shape[0] // 2
    lane = lax.broadcasted_iota(jnp.int32, (rows, halves.shape[1]), 1)
    return jnp.where(lane < HEAD_DIM, halves[:rows], halves[rows:])


def attend_kernel(nz, q_ref, *refs):
    lats, (wk_ref, wv_ref, att_ref, key_ref, value_ref, prob_ref) = refs[:nz], refs[nz:]
    local = q_ref.shape[1]
    z = lax.axis_index("z")
    q2 = head_halves(q_ref[0] * BF16(HEAD_DIM**-0.5))
    wk, wv = wk_ref[...], wv_ref[...]
    scores = []
    for k in range(nz):
        lat = lats[k][0]
        key = dot(lat, wk).astype(BF16)
        value = dot(lat, wv).astype(BF16)
        key_ref[0, k * local : (k + 1) * local] = key
        value_ref[0, k * local : (k + 1) * local] = value
        block = dot(q2, key, COLS)
        if k == 0:
            row = lax.rem(lax.broadcasted_iota(jnp.int32, block.shape, 0), local)
            column = lax.broadcasted_iota(jnp.int32, block.shape, 1)
            block = jnp.where(column <= row, block, -1e30)
        else:
            block = block + jnp.where(z >= k, 0.0, -1e30)
        scores.append(block)
    top = scores[0]
    for block in scores[1:]:
        top = jnp.maximum(top, block)
    top = jnp.max(top, axis=1, keepdims=True)
    exps = [jnp.exp(block - top) for block in scores]
    total = exps[0]
    for block in exps[1:]:
        total = total + block
    inverse = 1.0 / jnp.sum(total, axis=1, keepdims=True)
    mixed = jnp.zeros((2 * local, q_ref.shape[2]), F32)
    for k in range(nz):
        prob = (exps[k] * inverse).astype(BF16)
        prob_ref[0, 0, k] = prob
        mixed = mixed + dot(prob, value_ref[0, k * local : (k + 1) * local])
    att_ref[0] = join_halves(mixed).astype(BF16)


def attend(queries, lats, key_up, value_up):
    seqs, local, width = queries.shape
    nz = len(lats)
    pairs = width // 128
    query_spec = pl.BlockSpec((1, local, 128), lambda s, h: (s, 0, h))
    full_spec = pl.BlockSpec((1, nz * local, 128), lambda s, h: (s, 0, h))
    lat_spec = pl.BlockSpec((1, local, LATENT), lambda s, h: (s, 0, 0))
    up_spec = pl.BlockSpec((LATENT, 128), lambda s, h: (0, h))
    full = jax.ShapeDtypeStruct((seqs, nz * local, width), BF16)
    return pl.pallas_call(
        lambda *refs: attend_kernel(nz, *refs),
        grid=(seqs, pairs),
        in_specs=[query_spec] + [lat_spec] * nz + [up_spec] * 2,
        out_specs=[
            query_spec,
            full_spec,
            full_spec,
            pl.BlockSpec((1, 1, nz, 2 * local, local), lambda s, h: (s, h, 0, 0, 0)),
        ],
        out_shape=[
            jax.ShapeDtypeStruct(queries.shape, BF16),
            full,
            full,
            jax.ShapeDtypeStruct((seqs, pairs, nz, 2 * local, local), BF16),
        ],
        compiler_params=pltpu.CompilerParams(vmem_limit_bytes=48 * 2**20),
        cost_estimate=cost("c_attend", 16e9),
        name="attend",
    )(queries, *lats, key_up, value_up)


def attend_back_kernel(nz, pairs, first, q_ref, g_ref, att_ref, key_ref, value_ref, prob_ref, *refs):
    lats, (wk_ref, wv_ref, old_ref), rest = refs[:nz], refs[nz : nz + 3], refs[nz + 3 :]
    dq_ref, dlats, (up_ref, lat_acc) = rest[0], rest[1 : nz + 1], rest[nz + 1 :]
    pair = pl.program_id(0)
    local = q_ref.shape[1]
    scale = HEAD_DIM**-0.5
    grad = g_ref[0].astype(F32)
    query = head_halves(q_ref[0].astype(F32) * scale)
    g2 = head_halves(grad)
    inner = jnp.sum(head_halves(grad * att_ref[0].astype(F32)), axis=1, keepdims=True)
    query_t, g2_t = query.T.astype(BF16), g2.T.astype(BF16)
    g2 = g2.astype(BF16)
    dq = jnp.zeros((2 * local, 128), F32)
    up_key = jnp.zeros((128, LATENT), F32)
    up_value = jnp.zeros((128, LATENT), F32)
    for k in range(nz):
        rows = slice(k * local, (k + 1) * local)
        prob = prob_ref[0, 0, k]
        key, value = key_ref[0, rows], value_ref[0, rows]
        grad_prob = dot(g2, value, COLS)
        grad_score = (prob.astype(F32) * (grad_prob - inner)).astype(BF16)
        dq = dq + dot(grad_score, key)
        grad_key = dot(query_t, grad_score).astype(BF16)
        grad_value = dot(g2_t, prob).astype(BF16)
        term = dot(wk_ref[...], grad_key) + dot(wv_ref[...], grad_value)

        @pl.when(pair == 0)
        def _():
            lat_acc[:, rows] = term

        @pl.when(pair > 0)
        def _():
            lat_acc[:, rows] += term

        lat = lats[k][0]
        up_key = up_key + dot(grad_key, lat)
        up_value = up_value + dot(grad_value, lat)
    dq_ref[0] = (join_halves(dq) * scale).astype(BF16)
    up_ref[0, 0] = up_key.T if first else up_key.T + old_ref[0, 0]
    up_ref[1, 0] = up_value.T if first else up_value.T + old_ref[1, 0]

    @pl.when(pair == pairs - 1)
    def _():
        for k in range(nz):
            dlats[k][0] = lat_acc[:, k * local : (k + 1) * local].T.astype(BF16)


def attend_back(seq, queries, grad_att, attended, keys, values, probs, lats, key_up, value_up, old):
    _, local, width = queries.shape
    nz = len(lats)
    pairs = width // 128
    query_spec = pl.BlockSpec((1, local, 128), lambda h: (seq, 0, h))
    full_spec = pl.BlockSpec((1, nz * local, 128), lambda h: (seq, 0, h))
    lat_spec = pl.BlockSpec((1, local, LATENT), lambda h: (seq, 0, 0))
    up_spec = pl.BlockSpec((LATENT, 128), lambda h: (0, h))
    prob_spec = pl.BlockSpec((1, 1, nz, 2 * local, local), lambda h: (seq, h, 0, 0, 0))
    grad_spec = pl.BlockSpec((2, 1, LATENT, 128), lambda h: (0, h, 0, 0))
    outs = pl.pallas_call(
        lambda *refs: attend_back_kernel(nz, pairs, old is None, *refs),
        grid=(pairs,),
        in_specs=[query_spec] * 3
        + [full_spec] * 2
        + [prob_spec]
        + [lat_spec] * nz
        + [up_spec] * 2
        + [pl.BlockSpec(memory_space=pl.ANY) if old is None else grad_spec],
        out_specs=[pl.BlockSpec((1, local, 128), lambda h: (0, 0, h))]
        + [pl.BlockSpec((1, local, LATENT), lambda h: (0, 0, 0))] * nz
        + [grad_spec],
        out_shape=[jax.ShapeDtypeStruct((1, local, width), BF16)]
        + [jax.ShapeDtypeStruct((1, local, LATENT), BF16)] * nz
        + [jax.ShapeDtypeStruct((2, pairs, LATENT, 128), F32)],
        scratch_shapes=[pltpu.VMEM((LATENT, nz * local), F32)],
        compiler_params=pltpu.CompilerParams(vmem_limit_bytes=48 * 2**20),
        cost_estimate=cost("c_back", 17e9),
        name="attend_back",
    )(queries, grad_att, attended, keys, values, probs, *lats, key_up, value_up,
      key_up if old is None else old)
    return outs[0], outs[1 : nz + 1], outs[nz + 1]


VMEM = pl.BlockSpec(memory_space=pltpu.VMEM)
ANY = pl.BlockSpec(memory_space=pl.ANY)
PARAMS = pltpu.CompilerParams(vmem_limit_bytes=56 * 2**20)


def chunks(width):
    return [slice(start, min(start + 256, width)) for start in range(0, width, 256)]


def row_blocks(count, body):
    @pl.loop(0, count, step=64)
    def _(start):
        body(pl.ds(pl.multiple_of(start, 64), 64))


def block_copies(size, nz, sems, make):
    copies = []
    for b in range(size):
        for a in range(size):
            for k in range(nz):
                copies.append(make(b, a, k, sems.at[(b * size + a) * nz + k]))
    for copy in copies:
        copy.start()
    return copies


def mix_heads(attended, attn_w, first):
    rows, width = attended.shape
    depth = attn_w.shape[0]
    step = rows // 4

    def kernel(att_ref, w_ref, part_ref, sent_ref):
        part = dot(att_ref[...], w_ref[:, first : first + width], COLS)
        part_ref[...] = part
        sent_ref[...] = part.astype(BF16)

    return pl.pallas_call(
        kernel,
        grid=(4,),
        in_specs=[
            pl.BlockSpec((step, width), lambda i: (i, 0)),
            pl.BlockSpec(attn_w.shape, lambda i: (0, 0)),
        ],
        out_specs=[
            pl.BlockSpec((step, depth), lambda i: (i, 0)),
            pl.BlockSpec((step, depth), lambda i: ((i + 2) % 4, 0)),
        ],
        out_shape=[
            jax.ShapeDtypeStruct((rows, depth), F32),
            jax.ShapeDtypeStruct((rows, depth), BF16),
        ],
        compiler_params=PARAMS,
        cost_estimate=cost("c_mix", 2e9),
        name="mix_heads",
    )(attended, attn_w)


def feed_forward(tokens, partial, mixed, gain, grad_low, blocks, ring):
    size = len(blocks)
    nz, block_rows, wide = blocks[0][0].shape
    rows, depth = partial.shape
    width = wide // 2
    half_z = nz // 2
    down_rows = width // (half_z * size * size)
    direct = block_rows % 16 == 0 and down_rows % 16 == 0
    flat = [block for row in blocks for block in row]
    if not direct:
        flat = [merge_blocks(blocks, ring=ring)]

    def kernel(x_ref, part_ref, mix_ref, gain_ref, go_ref, *refs):
        sources, refs = refs[: len(flat)], refs[len(flat) :]
        resid_ref, norm_ref, w_ref, gate_ref, up_ref, hid_ref = refs[:6]
        outs, (grad_ref, in_sems, out_sems) = refs[6:-3], refs[-3:]

        def fetch(b, a, k, sem):
            away = k * (2 * lax.axis_index("core") - 1) if ring else -k
            z, y, x = place(size, nz, away, -b, -a)
            start = ((z * size + y) * size + x) * block_rows
            target = w_ref.at[pl.ds(pl.multiple_of(start, 16), block_rows)]
            return pltpu.make_async_copy(sources[b * size + a].at[k], target, sem)

        if direct:
            copies = block_copies(size, nz, in_sems, fetch)
        else:
            copies = [pltpu.make_async_copy(sources[0], w_ref, in_sems.at[0])]
            copies[0].start()

        def norm(at):
            resid = x_ref[at].astype(F32) + part_ref[at] + mix_ref[at].astype(F32)
            resid_ref[at] = resid
            norm_ref[at] = (resid * inverse_rms(resid) * gain_ref[...]).astype(BF16)

        row_blocks(rows, norm)
        for copy in copies:
            copy.wait()
        normed = norm_ref[...]
        low = go_ref[...]
        for at in chunks(width):
            gate = dot(normed, w_ref[:, at])
            up = dot(normed, w_ref[:, width + at.start : width + at.stop])
            gate_ref[:, at] = gate
            up_ref[:, at] = up
            hidden = (gate * jax.nn.sigmoid(gate) * up).astype(BF16)
            hid_ref[:, at] = hidden
            grad_ref[at] = dot(hidden, low, ROWS).astype(BF16)

        def leave(b, a, k, sem):
            _, y, x = place(size, nz, 0, b, a)
            start = ((k * size + y) * size + x) * down_rows
            source = grad_ref.at[pl.ds(pl.multiple_of(start, 16), down_rows)]
            return pltpu.make_async_copy(source, outs[b].at[a, k], sem)

        if direct:
            copies = block_copies(size, half_z, out_sems, leave)
        else:
            copies = [pltpu.make_async_copy(grad_ref, outs[0], out_sems.at[0])]
            copies[0].start()
        for copy in copies:
            copy.wait()

    outs = pl.pallas_call(
        kernel,
        in_specs=[VMEM] * 5 + [ANY] * len(flat),
        out_specs=[VMEM] * 6 + [ANY] * (size if direct else 1),
        out_shape=[
            jax.ShapeDtypeStruct((rows, depth), F32),
            jax.ShapeDtypeStruct((rows, depth), BF16),
            jax.ShapeDtypeStruct((depth, wide), BF16),
            jax.ShapeDtypeStruct((rows, width), F32),
            jax.ShapeDtypeStruct((rows, width), F32),
            jax.ShapeDtypeStruct((rows, width), BF16),
        ]
        + (
            [jax.ShapeDtypeStruct((size, half_z, down_rows, depth), BF16)] * size
            if direct
            else [jax.ShapeDtypeStruct((width, depth), BF16)]
        ),
        scratch_shapes=[
            pltpu.VMEM((width, depth), BF16),
            pltpu.SemaphoreType.DMA((nz * size * size,)),
            pltpu.SemaphoreType.DMA((half_z * size * size,)),
        ],
        compiler_params=PARAMS,
        cost_estimate=cost("c_ff", 14e9),
        name="feed_forward",
    )(tokens, partial, mixed, gain, grad_low, *flat)
    parts = list(outs[6:]) if direct else split_blocks(outs[6], half_z, True)
    return (*outs[:6], list(parts))


def feed_back(gate, up, hidden, normed, grad_low, blocks):
    size = len(blocks)
    half_z, block_rows, depth = blocks[0][0].shape
    nz = half_z * 2
    rows, width = gate.shape
    wide = 2 * width
    local = rows // 2
    grad_rows = depth // (nz * size * size)
    direct = block_rows % 16 == 0 and grad_rows % 16 == 0
    flat = [block for row in blocks for block in row]
    if not direct:
        flat = [merge_blocks(blocks, True)]

    def kernel(gate_ref, up_ref, hid_ref, norm_ref, go_ref, *refs):
        sources, refs = refs[: len(flat)], refs[len(flat) :]
        grad_ref, own_ref, sent_ref = refs[:3]
        outs, (w_ref, dw_ref, norm_t, acc_ref, in_sems, out_sems) = refs[3:-6], refs[-6:]

        def fetch(b, a, k, sem):
            _, y, x = place(size, nz, 0, -b, -a)
            start = ((k * size + y) * size + x) * block_rows
            target = w_ref.at[pl.ds(pl.multiple_of(start, 16), block_rows)]
            return pltpu.make_async_copy(sources[b * size + a].at[k], target, sem)

        if direct:
            copies = block_copies(size, half_z, in_sems, fetch)
        else:
            copies = [pltpu.make_async_copy(sources[0], w_ref, in_sems.at[0])]
            copies[0].start()
        norm_t[...] = norm_ref[...].T
        for copy in copies:
            copy.wait()
        low = go_ref[...]
        for at in chunks(width):
            weights = w_ref[at]
            grad_hidden = dot(low, weights, COLS)
            gate = gate_ref[:, at]
            sigma = jax.nn.sigmoid(gate)
            grad_gate = grad_hidden * up_ref[:, at] * sigma * (1.0 + gate * (1.0 - sigma))
            grad_up = grad_hidden * (gate * sigma)
            other = slice(width + at.start, width + at.stop)
            grad_ref[:, at] = grad_gate.astype(BF16)
            grad_ref[:, other] = grad_up.astype(BF16)
            dw_ref[:, at] = dot(norm_t[...], grad_ref[:, at]).astype(BF16)
            dw_ref[:, other] = dot(norm_t[...], grad_ref[:, other]).astype(BF16)
            term = dot(hid_ref[:, at], weights)
            if at.start == 0:
                acc_ref[...] = term
            else:
                acc_ref[...] += term

        def leave(b, a, k, sem):
            z, y, x = place(size, nz, k, b, a)
            start = ((z * size + y) * size + x) * grad_rows
            source = dw_ref.at[pl.ds(pl.multiple_of(start, 16), grad_rows)]
            return pltpu.make_async_copy(source, outs[b].at[a, k], sem)

        if direct:
            copies = block_copies(size, nz, out_sems, leave)
        else:
            copies = [pltpu.make_async_copy(dw_ref, outs[0], out_sems.at[0])]
            copies[0].start()
        own_ref[...] = acc_ref[:local]
        sent_ref[...] = acc_ref[local:].astype(BF16)
        for copy in copies:
            copy.wait()

    outs = pl.pallas_call(
        kernel,
        in_specs=[VMEM] * 5 + [ANY] * len(flat),
        out_specs=[VMEM] * 3 + [ANY] * (size if direct else 1),
        out_shape=[
            jax.ShapeDtypeStruct((rows, wide), BF16),
            jax.ShapeDtypeStruct((local, depth), F32),
            jax.ShapeDtypeStruct((local, depth), BF16),
        ]
        + (
            [jax.ShapeDtypeStruct((size, nz, grad_rows, wide), BF16)] * size
            if direct
            else [jax.ShapeDtypeStruct((depth, wide), BF16)]
        ),
        scratch_shapes=[
            pltpu.VMEM((width, depth), BF16),
            pltpu.VMEM((depth, wide), BF16),
            pltpu.VMEM((depth, rows), BF16),
            pltpu.VMEM((rows, depth), F32),
            pltpu.SemaphoreType.DMA((half_z * size * size,)),
            pltpu.SemaphoreType.DMA((nz * size * size,)),
        ],
        compiler_params=PARAMS,
        cost_estimate=cost("c_fb", 18e9),
        name="feed_back",
    )(gate, up, hidden, normed, grad_low, *flat)
    parts = outs[3:] if direct else split_blocks(outs[3], nz)
    return outs[0], outs[1], outs[2], list(parts)


def resid_back(normed_part, received, resid, grad_out, gain, attended, attn_w, first):
    rows, depth = resid.shape
    width = attended.shape[1]

    def kernel(part_ref, recv_ref, resid_ref, go_ref, gain_ref, att_ref, w_ref, grad_ref, datt_ref, dw_ref, dg_ref, low_ref):
        dg_ref[...] = jnp.zeros_like(dg_ref)

        def norm(at):
            resid = resid_ref[at]
            part = part_ref[at]
            inverse = inverse_rms(resid)
            scaled = resid * inverse
            dg_ref[...] += jnp.sum(part * scaled, axis=0, keepdims=True)
            weighted = (part + recv_ref[at].astype(F32)) * gain_ref[...]
            mean = jnp.mean(weighted * scaled, axis=-1, keepdims=True)
            grad = go_ref[at] + inverse * (weighted - scaled * mean)
            grad_ref[at] = grad
            low_ref[at] = grad.astype(BF16)

        row_blocks(rows, norm)
        low = low_ref[...]
        datt_ref[...] = dot(low, w_ref[:, first : first + width]).astype(BF16)
        dw_ref[...] = dot(low, att_ref[...], ROWS).astype(BF16)

    return pl.pallas_call(
        kernel,
        in_specs=[VMEM] * 7,
        out_specs=[VMEM] * 4,
        out_shape=[
            jax.ShapeDtypeStruct((rows, depth), F32),
            jax.ShapeDtypeStruct((rows, width), BF16),
            jax.ShapeDtypeStruct((depth, width), BF16),
            jax.ShapeDtypeStruct((1, depth), F32),
        ],
        scratch_shapes=[pltpu.VMEM((rows, depth), BF16)],
        compiler_params=PARAMS,
        cost_estimate=cost("c_rb", 4e9),
        name="resid_back",
    )(normed_part, received, resid, grad_out, gain, attended, attn_w)


def half(values, which, axis=1):
    size = values.shape[axis] // 2
    return lax.dynamic_slice_in_dim(values, which * size, size, axis)


def in_order(core, own, other, axis):
    return jnp.where(
        core == 0,
        jnp.concatenate([own, other], axis=axis),
        jnp.concatenate([other, own], axis=axis),
    )


def rms_back(grad_normed, inputs, inv_rms, gain):
    weighted = grad_normed * gain
    return inv_rms * weighted - inputs * inv_rms**3 * jnp.mean(
        weighted * inputs, axis=-1, keepdims=True
    )


def inverse_rms(values):
    return lax.rsqrt(jnp.mean(values * values, axis=-1, keepdims=True) + EPSILON)


def on_device(
    tokens,
    cotangent,
    group_ids,
    loss_weight,
    gain_attn,
    w_query,
    w_latent,
    w_key_up,
    w_value_up,
    w_out,
    gain_mlp,
    w_gate,
    w_up,
    w_down,
):
    nz, ny, nx = lax.axis_size("z"), lax.axis_size("y"), lax.axis_size("x")
    core = lax.axis_index("core")
    other = 1 - core
    local, depth = tokens.shape[1:]
    latent_width = w_latent.shape[1] // 2
    hidden_width = w_gate.shape[1] // 2
    query_width = w_query.shape[1] // 2
    gain_one = gain_attn.astype(F32)
    gain_two = gain_mlp.astype(F32)

    out_t = w_out.T
    row_parts = [w_query, w_latent, out_t, w_gate, w_up]
    mine = [half(part, core) for part in row_parts]
    theirs = [half(part, other) for part in row_parts]
    attn_recv = swap(jnp.concatenate(theirs[:3], axis=1))
    ff_recv = swap(jnp.concatenate(theirs[3:], axis=1))
    down_recv = to_half(w_down, 0)
    both = swap(jnp.concatenate([tokens, cotangent], axis=0))
    onehot = (group_ids[:, None] == jnp.arange(GROUPS, dtype=jnp.int32)[None, :]).astype(F32)
    onehot_other = swap(onehot)
    attn_shard = in_order(core, jnp.concatenate(mine[:3], axis=1), attn_recv, 0)
    ff_shard = in_order(core, jnp.concatenate(mine[3:], axis=1), ff_recv, 0)
    down_chip = in_order(core, w_down, down_recv, 0)

    counts = jnp.sum(onehot, axis=0) + jnp.sum(onehot_other, axis=0)
    counts = all_sum(counts, ("x", "y"))
    attn_shard = tie("attn_z", attn_shard, both, ff_shard, down_chip, onehot_other)
    attn_z = spread_z(attn_shard)
    attn_stack = tie("attn_plane", jnp.stack(attn_z), counts, ff_shard, down_chip)
    attn_a, attn_b = spread_own(attn_stack)
    attn_blocks = spread_rest(attn_stack, attn_a, attn_b)
    ff_shard = tie("ff_z", ff_shard, attn_z, counts)
    ff_z = spread_ring(ff_shard) if OPT.get("ring", 0) else spread_z(ff_shard)
    ff_stack = tie("ff_plane", jnp.stack(ff_z), attn_a, attn_b, attn_blocks[-1][-1])
    ff_a, ff_b = spread_own(ff_stack)

    tokens_both = jnp.concatenate([tokens[0], both[0]], axis=0)
    inputs = tokens_both.astype(F32)
    inv_one = inverse_rms(inputs)
    normed_one = (inputs * inv_one * gain_one).astype(BF16)
    total_seqs = ny * nx * 2 * group_ids.shape[0]

    def factor(row):
        return jnp.sum(row * loss_weight) * (total_seqs / GROUPS) / jnp.sum(row * counts)

    grad_out = jnp.concatenate(
        [
            cotangent[0].astype(F32) * factor(onehot[0]),
            both[1].astype(F32) * factor(onehot_other[0]),
        ],
        axis=0,
    )
    grad_out_low = grad_out.astype(BF16)

    attn_w = merge_blocks(attn_blocks)
    query_w = attn_w[:, :query_width]
    latent_w = attn_w[:, query_width : query_width + latent_width]
    latent = dot(normed_one, latent_w).astype(BF16).reshape(2, local, latent_width)
    latent = tie("lat", latent, ff_z, ff_a, ff_b)
    key_up = lax.dynamic_index_in_dim(w_key_up, core, 0, keepdims=False)
    value_up = lax.dynamic_index_in_dim(w_value_up, core, 0, keepdims=False)
    lats = [latent] + [
        lax.ppermute(latent, "z", [(i, i + k) for i in range(nz - k)]) for k in range(1, nz)
    ]
    ff_blocks = spread_rest(
        ff_stack, [tie("ff_rest", part, lats, attn_blocks[-1][-1]) for part in ff_a], ff_b
    )
    ff_last = ff_blocks[-1][-1]
    down_z = spread_down_z(tie("down_z", down_chip, ff_z, lats, (ff_a, ff_b), ff_last))
    down_own = tie("down_plane", down_stack(down_z), (ff_a, ff_b), ff_last)
    down_a, down_b = spread_own(down_own)
    down_blocks = spread_rest(down_own, down_a, down_b)
    down_last = down_blocks[-1][-1]
    queries = dot(normed_one, query_w).astype(BF16).reshape(2, local, query_width)
    queries = tie("attend", queries, (ff_a, ff_b), down_z, ff_last)
    attended, keys, values, probs = attend(queries, lats, key_up, value_up)
    attended_flat = tie("post", attended, (ff_a, ff_b), ff_last, down_z, (down_a, down_b))
    attended_flat = attended_flat.reshape(2 * local, query_width)
    first = query_width + latent_width
    partial, sent = mix_heads(attended_flat, attn_w, first)
    mixed = swap(sent)

    mixed = tie("gate", mixed, down_z, (down_a, down_b), down_last)
    resid, normed_two, ff_w, gate, up_value, hidden, down_parts = feed_forward(
        tokens_both, partial, mixed, gain_two[None], grad_out_low, ff_blocks, bool(OPT.get("ring", 0))
    )
    hidden = tie("hidden", hidden, (down_a, down_b), down_last)
    down_recv = send_b(down_parts)
    gate = tie("down_w", gate, down_parts, down_last)
    grad_ff, mlp_own, mlp_sent, ff_parts = feed_back(
        gate, up_value, hidden, normed_two, grad_out_low, down_blocks
    )
    ff_recv = send_b(ff_parts)
    down_row = add_b(down_parts, down_recv)
    down_recv_a = send_a(down_row)
    normed_part = dot(tie("normed_part", grad_ff, ff_parts, down_recv), ff_w, COLS)
    received = swap(
        jnp.concatenate([normed_part[local:], normed_part[:local]], axis=0).astype(BF16)
    )
    grad_resid, grad_attended, out_rows, gain_two_part = resid_back(
        normed_part, received, resid, grad_out, gain_two[None], attended_flat, attn_w, first
    )
    gain_two_part = gain_two_part[0]

    grad_attended = grad_attended.reshape(2, local, query_width)
    down_own = add_a(down_row, down_recv_a)
    down_recv_z = send_down_z(tie("down_back_z", down_own, grad_attended))
    grad_attended = tie(
        "back_0", grad_attended, down_recv, ff_parts, down_recv_a, out_rows, down_row, down_own, ff_recv
    )
    query_0, lat_0, up_0 = attend_back(
        0, queries, grad_attended, attended, keys, values, probs, lats, key_up, value_up, None
    )
    ff_row = add_b(ff_parts, ff_recv)
    ff_recv_a = send_a(ff_row)
    ff_own = add_a(ff_row, ff_recv_a)
    grad_attended = tie(
        "back_1",
        grad_attended,
        query_0,
        down_recv_a,
        ff_recv,
        down_recv_z,
        ff_row,
        down_own,
        ff_own,
    )
    query_1, lat_1, kv_grads = attend_back(
        1, queries, grad_attended, attended, keys, values, probs, lats, key_up, value_up, up_0
    )
    gate_own, up_own = ff_own[:, :, :hidden_width], ff_own[:, :, hidden_width:]
    gate_recv_z = send_z(gate_own)
    lat_1 = tie("lat_back", list(lat_1), ff_recv, ff_row, ff_recv_a, down_recv_z, gate_recv_z)
    lat_sum = jnp.concatenate([lat_0[0], lat_1[0]], axis=0).astype(F32)
    lat_recv = []
    for k in range(1, nz):
        sent = jnp.concatenate([lat_0[k], lat_1[k]], axis=0)
        lat_recv.append(lax.ppermute(sent, "z", [(i, i - k) for i in range(k, nz)]))
    kv_flat = kv_grads.reshape(depth, -1).astype(BF16)
    kv_parts = split_blocks(tie("kv", kv_flat, ff_recv, lat_1), nz, True)
    kv_row = add_b(kv_parts, send_b(kv_parts))
    kv_own = add_a(kv_row, send_a(kv_row))
    grad_queries = jnp.concatenate([query_0[0], query_1[0]], axis=0)
    grad_queries = tie("query_back", grad_queries, ff_recv_a, lat_1, ff_own)
    query_rows = dot(normed_one, grad_queries, ROWS).astype(BF16)
    attn_parts = split_blocks(jnp.concatenate([query_rows, out_rows], axis=1), nz)
    attn_parts = tie("attn_back", list(attn_parts), ff_recv_a, kv_own, down_recv_z)
    attn_recv = send_b(attn_parts)
    attn_row = add_b(attn_parts, attn_recv)
    attn_recv_a = send_a(attn_row)
    attn_own = add_a(attn_row, attn_recv_a)
    up_recv_z = send_z(tie("ff_back_z", up_own, lat_recv, down_recv_z, kv_row, attn_recv))
    kv_z = tie("kv_z", kv_own, lat_recv, attn_recv, up_recv_z)
    kv_recv = [shift(kv_z, "z", k) for k in range(1, nz)]
    attn_recv_z = send_z(tie("attn_back_z", attn_own, up_recv_z, kv_recv, lat_recv))
    for part in lat_recv:
        lat_sum = lat_sum + part.astype(F32)
    grad_latent = lat_sum.astype(BF16)
    grad_latent = tie(
        "grad_latent", grad_latent, attn_recv, ff_recv_a, ff_own, down_recv_z, kv_row, kv_own
    ).reshape(2 * local, latent_width)
    normed_query = dot(tie("normed_query", grad_queries, attn_parts, lat_1), query_w, COLS)
    last_parts = split_blocks(dot(normed_one, grad_latent, ROWS).astype(BF16), nz)
    last_parts = tie("last_back", list(last_parts), attn_recv, attn_recv_a, up_recv_z, normed_query)
    last_recv = send_b(last_parts)
    last_row = add_b(last_parts, last_recv)
    last_recv_a = send_a(last_row)
    last_own = add_a(last_row, last_recv_a)
    last_recv_z = send_z(tie("last_back_z", last_own, up_recv_z, kv_recv, attn_recv_z))
    normed_part = normed_query + dot(
        tie("normed_last", grad_latent, last_parts, up_recv_z), latent_w, COLS
    )
    gain_one_part = jnp.sum(normed_part * inputs * inv_one, axis=0)
    gains = jnp.stack([gain_one_part, gain_two_part])
    gains = tie("gains", gains, last_parts, last_recv, attn_recv_a, up_recv_z, kv_recv)
    gains = all_sum(gains, ("core", "x", "y", "z"))
    grad_normed = normed_part[:local] + swap(normed_part[local:].astype(BF16)).astype(F32)
    input_grad = (
        grad_resid[:local] + rms_back(grad_normed, inputs[:local], inv_one[:local], gain_one)
    ).astype(BF16)[None]
    mlp_sent = tie("mlp", mlp_sent, ff_parts, grad_attended, attn_parts)
    result = (resid[:local] + mlp_own + swap(mlp_sent).astype(F32)).astype(BF16)[None]
    kv_sum = kv_z.astype(F32)
    for part in kv_recv:
        kv_sum = kv_sum + part.astype(F32)
    kv_sum = tie("kv_spread", kv_sum.astype(BF16), last_parts, attn_recv, attn_recv_a)
    kv_a, kv_b = spread_own(kv_sum)
    kv_all = merge_blocks(spread_rest(kv_sum, kv_a, kv_b), fixed=True)
    kv_pair = in_order(core, kv_all[None], swap(kv_all)[None], 0).astype(F32)
    kv_pair = kv_pair.reshape((2,) + kv_grads.shape).transpose(1, 0, 3, 2, 4)
    kv_pair = kv_pair.reshape(2, KV_GROUPS, LATENT, query_width)

    def owned(totals):
        joined = jnp.concatenate(totals, axis=1).astype(BF16)
        received = swap(half(joined, other, 0))
        mine = half(joined, core, 0)
        results, start = [], 0
        for total in totals:
            width = total.shape[1]
            results.append(
                in_order(core, mine[:, start : start + width], received[:, start : start + width], 1)
                .astype(F32)
            )
            start += width
        return results

    owned_gate, owned_up = owned([add_z(gate_own, gate_recv_z), add_z(up_own, up_recv_z)])
    owned_down = own_down(down_own, tie("down_last", down_recv_z, attn_recv, lat_recv))
    attn_total = add_z(attn_own, attn_recv_z)
    owned_query, owned_out = owned([attn_total[:, :query_width], attn_total[:, query_width:]])
    (owned_latent,) = owned([add_z(last_own, last_recv_z)])
    return (
        result,
        input_grad,
        gains[0],
        owned_query,
        owned_latent,
        kv_pair[0],
        kv_pair[1],
        owned_out.T,
        gains[1],
        owned_gate,
        owned_up,
        owned_down,
    )


def solution(mesh):
    nz = mesh.shape["seq"]
    chips = mesh.shape["batch"] // 2
    nx = math.isqrt(chips)
    while chips % nx:
        nx -= 1
    fine = Mesh(mesh.devices.reshape(nz, chips // nx, nx, 2), ("z", "y", "x", "core"))
    batch = ("y", "x", "core")
    every = ("z",) + batch
    by_rows = P(every, None)
    in_specs = (
        P(batch, "z", None),
        P(batch, "z", None),
        P(batch),
        P(),
        P(),
        by_rows,
        by_rows,
        P(),
        P(),
        P(None, every),
        P(),
        by_rows,
        by_rows,
        by_rows,
    )
    out_specs = (
        P(batch, "z", None),
        P(batch, "z", None),
        P(),
        by_rows,
        by_rows,
        P(),
        P(),
        P(None, every),
        P(),
        by_rows,
        by_rows,
        by_rows,
    )
    return jax.shard_map(
        on_device, mesh=fine, in_specs=in_specs, out_specs=out_specs, check_vma=False
    )
```

time: 1230 us -> 402 us (0.33)
  Pallas kernels: 781 us -> 108 us
  waiting for transfers between devices: 159 us -> 106 us
  starting transfers between devices: 151 us -> 108 us
  matrix products: 39.4 us -> 11.2 us
  other arithmetic: 44.8 us -> 28.8 us
    pallas_call x14 -> x11, Pallas kernels: 765 us -> 92.1 us  [the longest x2 32.7 us: attend_back(): pl.pallas_call(lambda *refs: attend_back_kernel(nz, pairs, old is None, *...]
    ppermute x95 -> x41, waiting for transfers between devices: 143 us -> 68.1 us  [shift(): lax.ppermute(values, axis, [(i, (i + step) % size) for i in range(size)])]
    ppermute x95 -> x41, starting transfers between devices: 140 us -> 68.8 us  [shift(): lax.ppermute(values, axis, [(i, (i + step) % size) for i in range(size)])]
    ppermute x3 -> x33, starting transfers between devices: 4.42 us -> 33.8 us  [the longest x22 17.9 us: leg(): return lax.ppermute(values, PLANE, pairs)]
    dot_general x18 -> x7, matrix products: 39.4 us -> 11.2 us  [dot(): return lax.dot_general(a, b, dims, preferred_element_type=F32)]
    ppermute x3 -> x33, waiting for transfers between devices: 0.01 us -> 20.1 us  [the longest x22 20.1 us: leg(): return lax.ppermute(values, PLANE, pairs)]
  transfers between devices with their start and end apart: 101 -> 77, of which waited for: 31 -> 28; matrix products, arithmetic and copies ran while one was open for 8% -> 11% of each run, Pallas kernels for 64% -> 27%
where the time goes in v2:
time: 402 us; the launch traced here: 394 us
  starting transfers between devices  108 us (27%)
  Pallas kernels  108 us (27%)
  waiting for transfers between devices  106 us (26%)
  other arithmetic  28.8 us (7%)
  local copies, waits for them, and re-layouts  26.5 us (7%)
  matrix products  11.2 us (3%)
  between operations  5.49 us (1%)
    ppermute x41, starting transfers between devices, shift(): lax.ppermute(values, axis, [(i, (i + step) % size) for i in range(size)])  68.8 us
    ppermute x41, waiting for transfers between devices, shift(): lax.ppermute(values, axis, [(i, (i + step) % size) for i in range(size)])  68.1 us
    pallas_call x2, Pallas kernels, attend_back(): pl.pallas_call(lambda *refs: attend_back_kernel(nz, pairs, old is None, *...  32.7 us
    ppermute x22, waiting for transfers between devices, leg(): return lax.ppermute(values, PLANE, pairs)  20.1 us
    pallas_call x1, Pallas kernels, feed_forward(): pl.pallas_call(kernel, in_specs=[VMEM] * 5 + [ANY] * len(flat), out_specs...  18.3 us
    pallas_call x1, Pallas kernels, feed_back(): pl.pallas_call(kernel, in_specs=[VMEM] * 5 + [ANY] * len(flat), out_specs...  18.2 us
    ppermute x22, starting transfers between devices, leg(): return lax.ppermute(values, PLANE, pairs)  17.9 us
    ppermute x3, waiting for transfers between devices, on_device(): lax.ppermute(latent, 'z', [(i, i + k) for i in range(nz - k)])  17.6 us
  transfers between devices with their start and end apart: 77, of which 28 were waited for; matrix products, arithmetic and copies ran while one was open for 11% of the time, Pallas kernels for 27%

profile of v2, /device:TPU:9, one launch (start us, length us, event | category | flops | bytes accessed | tf_op | source)
XLA Modules:
  0.0 394.1 jit_solution(15836793025315794063)
XLA Ops:
  19.7 9.1 %collective-permute-done.5 = bf16[64,1280]{1,0:T(8,128)(2,1)S(1)} collective-permute-done((bf16[64,1280]{1,0:T(8,128)(2,1)S(1)}, bf16[64,1280]{1,0:T(8,128)(2,1)S(1)}, u32[]{:S(2)}, u32[]{:S(2)}) %collective-permute-start.5) | collective-permute-done | bytes 163872 | tf_op jit(solution)/shard_map/ppermute | solution.py:34
  28.8 4.0 %collective-permute-done.6 = bf16[64,1280]{1,0:T(8,128)(2,1)S(1)} collective-permute-done((bf16[64,1280]{1,0:T(8,128)(2,1)S(1)}, bf16[64,1280]{1,0:T(8,128)(2,1)S(1)}, u32[]{:S(2)}, u32[]{:S(2)}) %collective-permute-start.6) | collective-permute-done | bytes 163872 | tf_op jit(solution)/shard_map/ppermute | solution.py:34
  46.9 21.3 %collective-permute-done.18 = bf16[64,2816]{1,0:T(8,128)(2,1)} collective-permute-done((bf16[64,2816]{1,0:T(8,128)(2,1)}, bf16[64,2816]{1,0:T(8,128)(2,1)}, u32[]{:S(2)}, u32[]{:S(2)}) %collective-permute-start.18) | collective-permute-done | bytes 360480 | tf_op jit(solution)/shard_map/ppermute | solution.py:34
  82.5 3.7 merge.2
  95.6 14.9 %collective-permute-done.13.refs_3_.refs_8_ = bf16[2,256,256]{2,1,0:T(8,128)(2,1)S(1)} collective-permute-done((bf16[2,256,256]{2,1,0:T(8,128)(2,1)S(1)}, bf16[2,256,256]{2,1,0:T(8,128)(2,1)S(1)}, u32[]{:S(2)}, u32[]{:S(2)}) %collective-permute-start.13) | collective-permute-done | bytes 262176 | tf_op jit(solution)/shard_map/ppermute | solution.py:835
  115.1 16.0 %attend.1 = (bf16[2,256,512]{2,1,0:T(8,128)(2,1)S(1)}, bf16[2,1024,512]{2,1,0:T(8,128)(2,1)S(1)}, bf16[2,1024,512]{2,1,0:T(8,128)(2,1)}, bf16[2,4,4,512,256]{4,3,2,1,0:T(8,128)(2,1)}) custom-call(bf16[2,256,512]{2,1,0:T(8,128)(2,1)S(1)} %bitcast.183, bf16[2,256,256]{2,1,0:T(8,128)(2,1)S(1)} %bitcast.180, ...), custom_call_target="tpu_custom_call" | custom-call | flops 16000000000 | bytes 4096 | tf_op jit(solution)/shard_map/attend/pallas_call | solution.py:342
  133.3 5.4 %mix_heads.1 = (f32[512,1024]{1,0:T(8,128)}, bf16[512,1024]{1,0:T(8,128)(2,1)}) custom-call(bf16[512,512]{1,0:T(8,128)(2,1)} %bitcast.186, bf16[1024,1280]{1,0:T(8,128)(2,1)} %bitcast.169), custom_call_target="tpu_custom_call" | custom-call | flops 2000000000 | bytes 4096 | tf_op jit(solution)/shard_map/mix_heads/pallas_call | solution.py:481
  138.7 6.0 %collective-permute-start.15 = (bf16[512,1024]{1,0:T(8,128)(2,1)}, bf16[512,1024]{1,0:T(8,128)(2,1)}, u32[]{:S(2)}, u32[]{:S(2)}) collective-permute-start(bf16[512,1024]{1,0:T(8,128)(2,1)} %get-tuple-element.81), channel_id=1, source_target_pairs={{0,1},{1,0},{2,3},{3,2},{4,5},{5,4},{6,7},{7,6},{8,9},{9,8},{10,11... | collective-permute-start | bytes 3145736 | tf_op jit(solution)/shard_map/ppermute | solution.py:34
  158.1 18.3 %feed_forward.1 = (f32[512,1024]{1,0:T(8,128)}, bf16[512,1024]{1,0:T(8,128)(2,1)}, bf16[1024,2816]{1,0:T(8,128)(2,1)}, f32[512,1408]{1,0:T(8,128)}, f32[512,1408...) custom-call(bf16[512,1024]{1,0:T(8,128)(2,1)} %get-tuple-element.159, ...), custom_call_target="tpu_custom_call" | custom-call | flops 14000000000 | bytes 4096 | tf_op jit(solution)/shard_map/feed_forward/pallas_call | solution.py:565
  177.6 18.2 %feed_back.1 = (bf16[512,2816]{1,0:T(8,128)(2,1)}, f32[256,1024]{1,0:T(8,128)}, bf16[256,1024]{1,0:T(8,128)(2,1)}, bf16[2,4,64,2816]{3,2,1,0:T(8,128)(2,1)}, bf16[2,4,64,2816]{3,2,1,0:T(8,128)(2,1)}) custom-call(f32[512,1408]{1,0:T(8,128)} %get-tuple-element.85.gate_ref, f32[512,1408]{1,0:T(8,128)} %get-tuple-element.86.up_ref, ...), custom_call_target="tpu_custom_call" | custom-call | flops 17999998976 | bytes 4096 | tf_op jit(solution)/shard_map/feed_back/pallas_call | solution.py:662
  201.3 7.2 %fusion.44 = (bf16[512,1024]{1,0:T(8,128)(2,1)S(1)}, f32[512,1024]{1,0:T(8,128)}) fusion(bf16[512,2816]{1,0:T(8,128)(2,1)S(1)} %copy-done.64, bf16[1024,2816]{1,0:T(8,128)(2,1)} %get-tuple-element.98), kind=kOutput, calls=%fused_computation.168 | convolution fusion | flops 2953314304 | bytes 11796480 | tf_op jit(solution)/shard_map/dot_general | solution.py:26
  212.3 3.3 collective-permute-done.32
  221.2 8.3 %resid_back.1 = (f32[512,1024]{1,0:T(8,128)}, bf16[512,512]{1,0:T(8,128)(2,1)}, bf16[1024,512]{1,0:T(8,128)(2,1)}, f32[1,1024]{1,0:T(1,128)}) custom-call(f32[512,1024]{1,0:T(8,128)} %get-tuple-element.197.part_ref, bf16[512,1024]{1,0:T(8,128)(2,1)} %copy-done.60, f32[512,1024]{1,0:T(8,128)} %get-tuple-element.84.resid_ref, ...), custom_call_target="tpu_custom_call" | custom-call | flops 4000000000 | bytes 4096 | tf_op jit(solution)/shard_map/resid_back/pallas_call | solution.py:716
  229.4 8.1 %collective-permute-done.33 = bf16[2,4,64,2816]{3,2,1,0:T(8,128)(2,1)} collective-permute-done((bf16[2,4,64,2816]{3,2,1,0:T(8,128)(2,1)}, bf16[2,4,64,2816]{3,2,1,0:T(8,128)(2,1)}, u32[]{:S(2)}, u32[]{:S(2)}) %collective-permute-start.33) | collective-permute-done | bytes 2883616 | tf_op jit(solution)/shard_map/ppermute | solution.py:50
  241.7 16.3 %attend_back.2 = (bf16[1,256,512]{2,1,0:T(8,128)(2,1)S(1)}, bf16[1,256,256]{2,1,0:T(8,128)(2,1)S(1)}, bf16[1,256,256]{2,1,0:T(8,128)(2,1)S(1)}, bf16[1,256,256]{...) custom-call(bf16[2,256,512]{2,1,0:T(8,128)(2,1)S(1)} %bitcast.184, ...), custom_call_target="tpu_custom_call" | custom-call | flops 16999999488 | bytes 4096 | tf_op jit(solution)/shard_map/attend_back/pallas_call | solution.py:421
  263.0 16.4 %attend_back.3 = (bf16[1,256,512]{2,1,0:T(8,128)(2,1)S(1)}, bf16[1,256,256]{2,1,0:T(8,128)(2,1)S(1)}, bf16[1,256,256]{2,1,0:T(8,128)(2,1)S(1)}, bf16[1,256,256]{...) custom-call(bf16[2,256,512]{2,1,0:T(8,128)(2,1)S(1)} %bitcast.185, ...), custom_call_target="tpu_custom_call" | custom-call | flops 16999999488 | bytes 4096 | tf_op jit(solution)/shard_map/attend_back/pallas_call | solution.py:421
  295.9 10.7 %collective-permute-start.73 = (bf16[64,1408]{1,0:T(8,128)(2,1)}, bf16[64,1408]{1,0:T(8,128)(2,1)S(1)}, u32[]{:S(2)}, u32[]{:S(2)}) collective-permute-start(bf16[64,1408]{1,0:T(8,128)(2,1)} %get-tuple-element.162), channel_id=1, source_target_pairs={{0,16},{8,24},{16,0},{24,8},{1,17},{9,25},{17,1},{25,9},{2,18},{10... | collective-permute-start | bytes 540680 | tf_op jit(solution)/shard_map/ppermute | solution.py:34
  315.3 5.3 %collective-permute-start.44 = (bf16[256,1024]{1,0:T(8,128)(2,1)S(1)}, bf16[256,1024]{1,0:T(8,128)(2,1)S(1)}, u32[]{:S(2)}, u32[]{:S(2)}) collective-permute-start(bf16[256,1024]{1,0:T(8,128)(2,1)S(1)} %slice.339), channel_id=1, source_target_pairs={{0,1},{1,0},{2,3},{3,2},{4,5},{5,4},{6,7},{7,6},{8,9},{9,8},{10,11... | collective-permute-start | bytes 1572872 | tf_op jit(solution)/shard_map/ppermute | solution.py:34
  322.0 4.0 %collective-permute-start.46 = (f32[2,1024]{1,0:T(2,128)S(1)}, f32[2,1024]{1,0:T(2,128)S(1)}, u32[]{:S(2)}, u32[]{:S(2)}) collective-permute-start(f32[2,1024]{1,0:T(2,128)S(1)} %pad_maximum_fusion.15), channel_id=1, source_target_pairs={{0,1},{1,0},{2,3},{3,2},{4,5},{5,4},{6,7},{7,6},{8,9},{9,8},{10,11... | collective-permute-start | bytes 24584 | tf_op jit(solution)/shard_map/ppermute | solution.py:34
  334.8 3.5 collective-permute-start.75
  348.5 4.0 %collective-permute-start.62 = (bf16[32,256]{1,0:T(8,128)(2,1)S(1)}, bf16[32,256]{1,0:T(8,128)(2,1)S(1)}, u32[]{:S(2)}, u32[]{:S(2)}) collective-permute-start(bf16[32,256]{1,0:T(8,128)(2,1)S(1)} %get-tuple-element.191), channel_id=1, source_target_pairs={{0,1},{1,0},{2,3},{3,2},{4,5},{5,4},{6,7},{7,6},{8,9},{9,8},{10,11... | collective-permute-start | bytes 49160 | tf_op jit(solution)/shard_map/ppermute | solution.py:34
  360.8 6.6 %collective-permute-done.66 = bf16[4,64,256]{2,1,0:T(8,128)(2,1)S(1)} collective-permute-done((bf16[4,64,256]{2,1,0:T(8,128)(2,1)S(1)}, bf16[4,64,256]{2,1,0:T(8,128)(2,1)S(1)}, u32[]{:S(2)}, u32[]{:S(2)}) %collective-permute-start.66) | collective-permute-done | bytes 131104 | tf_op jit(solution)/shard_map/ppermute | solution.py:34
  367.4 3.4 collective-permute-done.67
  377.3 6.4 %collective-permute-done.55 = bf16[64,1024]{1,0:T(8,128)(2,1)S(1)} collective-permute-done((bf16[64,1024]{1,0:T(8,128)(2,1)S(1)}, bf16[64,1024]{1,0:T(8,128)(2,1)S(1)}, u32[]{:S(2)}, u32[]{:S(2)}) %collective-permute-start.55) | collective-permute-done | bytes 131104 | tf_op jit(solution)/shard_map/ppermute | solution.py:34
  (381 shorter events, 168.2 us)
Async XLA Ops:
  36.9 31.2 %collective-permute-start.18 = (bf16[64,2816]{1,0:T(8,128)(2,1)}, bf16[64,2816]{1,0:T(8,128)(2,1)}, u32[]{:S(2)}, u32[]{:S(2)}) collective-permute-start(bf16[64,2816]{1,0:T(8,128)(2,1)} %maximum_select_fusion.2), channel_id=1, source_target_pairs={{0,16},{8,24},{16,0},{24,8},{1,17},{9,25},{17,1},{25,9},{2,18},{10... | collective-permute-start | bytes 1081352 | tf_op jit(solution)/shard_map/ppermute | solution.py:34
  38.3 32.4 %collective-permute-start.19 = (bf16[64,2816]{1,0:T(8,128)(2,1)}, bf16[64,2816]{1,0:T(8,128)(2,1)}, u32[]{:S(2)}, u32[]{:S(2)}) collective-permute-start(bf16[64,2816]{1,0:T(8,128)(2,1)} %maximum_select_fusion.2), channel_id=1, source_target_pairs={{0,24},{8,0},{16,8},{24,16},{1,25},{9,1},{17,9},{25,17},{2,26},{10... | collective-permute-start | bytes 1081352 | tf_op jit(solution)/shard_map/ppermute | solution.py:34
  42.8 30.5 %collective-permute-start.11 = (bf16[4,64,1280]{2,1,0:T(8,128)(2,1)S(1)}, bf16[4,64,1280]{2,1,0:T(8,128)(2,1)S(1)}, u32[]{:S(2)}, u32[]{:S(2)}) collective-permute-start(bf16[4,64,1280]{2,1,0:T(8,128)(2,1)S(1)} %collective-permute-done.9.refs_1_), channel_id=1, source_target_pairs={{0,4},{1,3},{2,6},{3,1},{4,0},{5,7},{6,2},{7,5},{8,12},{9,11},{10,... | collective-permute-start | bytes 1966088 | tf_op jit(solution)/shard_map/ppermute | solution.py:50
  44.7 33.7 %collective-permute-start.10 = (bf16[4,64,1280]{2,1,0:T(8,128)(2,1)S(1)}, bf16[4,64,1280]{2,1,0:T(8,128)(2,1)S(1)}, u32[]{:S(2)}, u32[]{:S(2)}) collective-permute-start(bf16[4,64,1280]{2,1,0:T(8,128)(2,1)S(1)} %pad_maximum_fusion.8.refs_0_), channel_id=1, source_target_pairs={{0,4},{1,3},{2,6},{3,1},{4,0},{5,7},{6,2},{7,5},{8,12},{9,11},{10,... | collective-permute-start | bytes 1966088 | tf_op jit(solution)/shard_map/ppermute | solution.py:50
  73.4 40.4 %collective-permute-start.20 = (bf16[4,64,2816]{2,1,0:T(8,128)(2,1)}, bf16[4,64,2816]{2,1,0:T(8,128)(2,1)}, u32[]{:S(2)}, u32[]{:S(2)}) collective-permute-start(bf16[4,64,2816]{2,1,0:T(8,128)(2,1)} %pad_maximum_fusion.2.refs_0_), channel_id=1, source_target_pairs={{0,2},{1,5},{2,0},{3,7},{4,6},{5,1},{6,4},{7,3},{8,10},{9,13},{10,... | collective-permute-start | bytes 4325384 | tf_op jit(solution)/shard_map/ppermute | solution.py:50
  78.0 80.1 %collective-permute-start.21 = (bf16[4,64,2816]{2,1,0:T(8,128)(2,1)}, bf16[4,64,2816]{2,1,0:T(8,128)(2,1)}, u32[]{:S(2)}, u32[]{:S(2)}) collective-permute-start(bf16[4,64,2816]{2,1,0:T(8,128)(2,1)} %pad_maximum_fusion.2.refs_0_), channel_id=1, source_target_pairs={{0,4},{1,3},{2,6},{3,1},{4,0},{5,7},{6,2},{7,5},{8,12},{9,11},{10,... | collective-permute-start | bytes 4325384 | tf_op jit(solution)/shard_map/ppermute | solution.py:50
  88.8 21.7 %collective-permute-start.13 = (bf16[2,256,256]{2,1,0:T(8,128)(2,1)S(1)}, bf16[2,256,256]{2,1,0:T(8,128)(2,1)S(1)}, u32[]{:S(2)}, u32[]{:S(2)}) collective-permute-start(bf16[2,256,256]{2,1,0:T(8,128)(2,1)S(1)} %bitcast.178), channel_id=1, source_target_pairs={{0,16},{8,24},{1,17},{9,25},{2,18},{10,26},{3,19},{11,27},{4,20},{... | collective-permute-start | bytes 786440 | tf_op jit(solution)/shard_map/ppermute | solution.py:835
  110.5 28.2 %collective-permute-start.23 = (bf16[176,1024]{1,0:T(8,128)(2,1)S(1)}, bf16[176,1024]{1,0:T(8,128)(2,1)S(1)}, u32[]{:S(2)}, u32[]{:S(2)}) collective-permute-start(bf16[176,1024]{1,0:T(8,128)(2,1)S(1)} %copy-done.40), channel_id=1, source_target_pairs={{0,8},{8,16},{17,25},{25,1},{2,10},{10,18},{19,27},{27,3},{4,12},{... | collective-permute-start | bytes 1081352 | tf_op jit(solution)/shard_map/ppermute | solution.py:145
  111.2 33.5 %collective-permute-start.24 = (bf16[176,1024]{1,0:T(8,128)(2,1)S(1)}, bf16[176,1024]{1,0:T(8,128)(2,1)S(1)}, u32[]{:S(2)}, u32[]{:S(2)}) collective-permute-start(bf16[176,1024]{1,0:T(8,128)(2,1)S(1)} %copy-done.40), channel_id=1, source_target_pairs={{0,16},{8,24},{17,1},{25,9},{2,18},{10,26},{19,3},{27,11},{4,20},{... | collective-permute-start | bytes 1081352 | tf_op jit(solution)/shard_map/ppermute | solution.py:145
  112.5 32.2 %collective-permute-start.25 = (bf16[176,1024]{1,0:T(8,128)(2,1)S(1)}, bf16[176,1024]{1,0:T(8,128)(2,1)S(1)}, u32[]{:S(2)}, u32[]{:S(2)}) collective-permute-start(bf16[176,1024]{1,0:T(8,128)(2,1)S(1)} %copy-done.40), channel_id=1, source_target_pairs={{0,24},{8,0},{17,9},{25,17},{2,26},{10,2},{19,11},{27,19},{4,28},{... | collective-permute-start | bytes 1081352 | tf_op jit(solution)/shard_map/ppermute | solution.py:145
  113.8 32.1 %collective-permute-start.22 = (bf16[4,64,2816]{2,1,0:T(8,128)(2,1)}, bf16[4,64,2816]{2,1,0:T(8,128)(2,1)S(1)}, u32[]{:S(2)}, u32[]{:S(2)}) collective-permute-start(bf16[4,64,2816]{2,1,0:T(8,128)(2,1)} %collective-permute-done.20.refs_1_), channel_id=1, source_target_pairs={{0,4},{1,3},{2,6},{3,1},{4,0},{5,7},{6,2},{7,5},{8,12},{9,11},{10,... | collective-permute-start | bytes 4325384 | tf_op jit(solution)/shard_map/ppermute | solution.py:50
  152.9 23.6 %collective-permute-start.27 = (bf16[2,176,1024]{2,1,0:T(8,128)(2,1)}, bf16[2,176,1024]{2,1,0:T(8,128)(2,1)S(1)}, u32[]{:S(2)}, u32[]{:S(2)}) collective-permute-start(bf16[2,176,1024]{2,1,0:T(8,128)(2,1)} %pad_maximum_fusion.7.refs_0_), channel_id=1, source_target_pairs={{0,4},{1,3},{2,6},{3,1},{4,0},{5,7},{6,2},{7,5},{8,12},{9,11},{10,... | collective-permute-start | bytes 2162696 | tf_op jit(solution)/shard_map/ppermute | solution.py:50
  156.7 19.8 %collective-permute-start.28 = (bf16[2,176,1024]{2,1,0:T(8,128)(2,1)}, bf16[2,176,1024]{2,1,0:T(8,128)(2,1)S(1)}, u32[]{:S(2)}, u32[]{:S(2)}) collective-permute-start(bf16[2,176,1024]{2,1,0:T(8,128)(2,1)} %collective-permute-done.26.refs_1_), channel_id=1, source_target_pairs={{0,4},{1,3},{2,6},{3,1},{4,0},{5,7},{6,2},{7,5},{8,12},{9,11},{10,... | collective-permute-start | bytes 2162696 | tf_op jit(solution)/shard_map/ppermute | solution.py:50
  176.4 20.9 %collective-permute-start.31 = (bf16[2,2,176,1024]{3,2,1,0:T(8,128)(2,1)}, bf16[2,2,176,1024]{3,2,1,0:T(8,128)(2,1)S(1)}, u32[]{:S(2)}, u32[]{:S(2)}) collective-permute-start(bf16[2,2,176,1024]{3,2,1,0:T(8,128)(2,1)} %get-tuple-element.102), channel_id=1, source_target_pairs={{0,4},{1,3},{2,6},{3,1},{4,0},{5,7},{6,2},{7,5},{8,12},{9,11},{10,... | collective-permute-start | bytes 4325384 | tf_op jit(solution)/shard_map/ppermute | solution.py:50
  195.8 41.7 %collective-permute-start.33 = (bf16[2,4,64,2816]{3,2,1,0:T(8,128)(2,1)}, bf16[2,4,64,2816]{3,2,1,0:T(8,128)(2,1)}, u32[]{:S(2)}, u32[]{:S(2)}) collective-permute-start(bf16[2,4,64,2816]{3,2,1,0:T(8,128)(2,1)} %get-tuple-element.96), channel_id=1, source_target_pairs={{0,4},{1,3},{2,6},{3,1},{4,0},{5,7},{6,2},{7,5},{8,12},{9,11},{10,... | collective-permute-start | bytes 8650760 | tf_op jit(solution)/shard_map/ppermute | solution.py:50
  216.8 42.8 %collective-permute-start.34 = (bf16[176,1024]{1,0:T(8,128)(2,1)S(1)}, bf16[176,1024]{1,0:T(8,128)(2,1)S(1)}, u32[]{:S(2)}, u32[]{:S(2)}) collective-permute-start(bf16[176,1024]{1,0:T(8,128)(2,1)S(1)} %get-tuple-element.165), channel_id=1, source_target_pairs={{8,0},{16,8},{25,17},{1,25},{10,2},{18,10},{27,19},{3,27},{12,4},{... | collective-permute-start | bytes 1081352 | tf_op jit(solution)/shard_map/ppermute | solution.py:175
  217.5 42.1 %collective-permute-start.35 = (bf16[176,1024]{1,0:T(8,128)(2,1)S(1)}, bf16[176,1024]{1,0:T(8,128)(2,1)S(1)}, u32[]{:S(2)}, u32[]{:S(2)}) collective-permute-start(bf16[176,1024]{1,0:T(8,128)(2,1)S(1)} %get-tuple-element.164), channel_id=1, source_target_pairs={{16,0},{24,8},{1,17},{9,25},{18,2},{26,10},{3,19},{11,27},{20,4},{... | collective-permute-start | bytes 1081352 | tf_op jit(solution)/shard_map/ppermute | solution.py:175
  218.8 40.8 %collective-permute-start.36 = (bf16[176,1024]{1,0:T(8,128)(2,1)S(1)}, bf16[176,1024]{1,0:T(8,128)(2,1)S(1)}, u32[]{:S(2)}, u32[]{:S(2)}) collective-permute-start(bf16[176,1024]{1,0:T(8,128)(2,1)S(1)} %get-tuple-element.163), channel_id=1, source_target_pairs={{24,0},{0,8},{9,17},{17,25},{26,2},{2,10},{11,19},{19,27},{28,4},{... | collective-permute-start | bytes 1081352 | tf_op jit(solution)/shard_map/ppermute | solution.py:175
  259.7 20.0 %collective-permute-start.38 = (bf16[64,1408]{1,0:T(8,128)(2,1)}, bf16[64,1408]{1,0:T(8,128)(2,1)}, u32[]{:S(2)}, u32[]{:S(2)}) collective-permute-start(bf16[64,1408]{1,0:T(8,128)(2,1)} %get-tuple-element.153), channel_id=1, source_target_pairs={{0,8},{8,16},{16,24},{24,0},{1,9},{9,17},{17,25},{25,1},{2,10},{10... | collective-permute-start | bytes 540680 | tf_op jit(solution)/shard_map/ppermute | solution.py:34
  259.8 20.0 %collective-permute-start.39 = (bf16[64,1408]{1,0:T(8,128)(2,1)}, bf16[64,1408]{1,0:T(8,128)(2,1)}, u32[]{:S(2)}, u32[]{:S(2)}) collective-permute-start(bf16[64,1408]{1,0:T(8,128)(2,1)} %get-tuple-element.152), channel_id=1, source_target_pairs={{0,16},{8,24},{16,0},{24,8},{1,17},{9,25},{17,1},{25,9},{2,18},{10... | collective-permute-start | bytes 540680 | tf_op jit(solution)/shard_map/ppermute | solution.py:34
  286.3 20.3 %collective-permute-start.63 = (bf16[2,4,64,256]{3,2,1,0:T(8,128)(2,1)S(1)}, bf16[2,4,64,256]{3,2,1,0:T(8,128)(2,1)S(1)}, u32[]{:S(2)}, u32[]{:S(2)}) collective-permute-start(bf16[2,4,64,256]{3,2,1,0:T(8,128)(2,1)S(1)} %get-tuple-element.135), channel_id=1, source_target_pairs={{0,4},{1,3},{2,6},{3,1},{4,0},{5,7},{6,2},{7,5},{8,12},{9,11},{10,... | collective-permute-start | bytes 786440 | tf_op jit(solution)/shard_map/ppermute | solution.py:50
  291.9 62.2 %collective-permute-start.52 = (bf16[2,4,64,1024]{3,2,1,0:T(8,128)(2,1)S(1)}, bf16[2,4,64,1024]{3,2,1,0:T(8,128)(2,1)S(1)}, u32[]{:S(2)}, u32[]{:S(2)}) collective-permute-start(bf16[2,4,64,1024]{3,2,1,0:T(8,128)(2,1)S(1)} %get-tuple-element.131), channel_id=1, source_target_pairs={{0,4},{1,3},{2,6},{3,1},{4,0},{5,7},{6,2},{7,5},{8,12},{9,11},{10,... | collective-permute-start | bytes 3145736 | tf_op jit(solution)/shard_map/ppermute | solution.py:50
  293.1 20.8 %collective-permute-start.72 = (bf16[64,1408]{1,0:T(8,128)(2,1)}, bf16[64,1408]{1,0:T(8,128)(2,1)S(1)}, u32[]{:S(2)}, u32[]{:S(2)}) collective-permute-start(bf16[64,1408]{1,0:T(8,128)(2,1)} %get-tuple-element.160), channel_id=1, source_target_pairs={{0,8},{8,16},{16,24},{24,0},{1,9},{9,17},{17,25},{25,1},{2,10},{10... | collective-permute-start | bytes 540680 | tf_op jit(solution)/shard_map/ppermute | solution.py:34
  315.3 40.4 %collective-permute-start.44 = (bf16[256,1024]{1,0:T(8,128)(2,1)S(1)}, bf16[256,1024]{1,0:T(8,128)(2,1)S(1)}, u32[]{:S(2)}, u32[]{:S(2)}) collective-permute-start(bf16[256,1024]{1,0:T(8,128)(2,1)S(1)} %slice.339), channel_id=1, source_target_pairs={{0,1},{1,0},{2,3},{3,2},{4,5},{5,4},{6,7},{7,6},{8,9},{9,8},{10,11... | collective-permute-start | bytes 1572872 | tf_op jit(solution)/shard_map/ppermute | solution.py:34
  (119 other events, 1101.9 us)
